TPU v7x, 32 devices: a whole 2x2x4 slice. The times are simulated.
32 devices in a mesh: seq: 4 (over y, core), ctx: 2 (over x), fsdp: 4 (over z).
Axes of the slice: x: 2, y: 2, z: 4, core: 2. Of those that a mesh axis runs over, the one named last changes fastest.
Arguments:
- tokens: bfloat16 [16, 1024, 960], P(('seq', 'fsdp'), 'ctx'), may hold values from -6 to 6
- cotangent: bfloat16 [16, 1024, 960], P(('seq', 'fsdp'), 'ctx'), may hold values from -6 to 6
- positions: int32 [16, 1024], P(('seq', 'fsdp'), 'ctx'), may hold values from 0 to 1535, as said below
- doc_ids: int32 [16, 8], P(('seq', 'fsdp')), may hold values from 0 to 3, as said below
- gain_attn: bfloat16 [960], P('fsdp'), may hold values from 0.099609375 to 1.8984375
- w_qkv: bfloat16 [960, 1600], P('fsdp'), may hold values from -0.25 to 0.25
- w_out: bfloat16 [960, 960], P('fsdp'), may hold values from -0.75 to 0.75
- gain_mlp: bfloat16 [960], P('fsdp'), may hold values from 0.099609375 to 1.8984375
- w_gate_up: bfloat16 [960, 5120], P('fsdp'), may hold values from -0.1875 to 0.1875
- w_down: bfloat16 [2560, 960], P('fsdp'), may hold values from -0.125 to 0.125
Outputs:
- output: bfloat16 [16, 1024, 960], P(('seq', 'fsdp'), 'ctx')
- input_grad: bfloat16 [16, 1024, 960], P(('seq', 'fsdp'), 'ctx')
- grad_gain_attn: float32 [960], P('fsdp')
- grad_w_qkv: float32 [960, 1600], P('fsdp')
- grad_w_out: float32 [960, 960], P('fsdp')
- grad_gain_mlp: float32 [960], P('fsdp')
- grad_w_gate_up: float32 [960, 5120], P('fsdp')
- grad_w_down: float32 [2560, 960], P('fsdp')
Inputs may be any that keep to these rules, and one draw needn't show every extreme that they name: In each sequence the positions start at 0 and rise by 1 or 2 from each token to the next, by 2 at exactly 512 of the steps, so the last position is the largest. `doc_ids`: in each sequence the document numbers start at 0 and rise by 0 or 1 from block to block; the last block holds the largest.
All inputs are finite; a program needn't handle non-finite values.
Results may differ from a plain program's by a relative error of at most 0.023.
Values may be sent and summed in bfloat16 or wider, within the bound.
No kernel may reach another device: no remote copies, remote signals or barrier semaphores. Data moves between devices by JAX's collectives and lax.ppermute only.
A program may use at most 192 MiB of HBM per device.

v0:
```python
import jax
import jax.numpy as jnp
from jax import lax
from jax.sharding import PartitionSpec as P

D = 960
HEADS = 15
KV_HEADS = 5
HEAD_DIM = 64
FF = 2560
BLK = 128
TOK_DEV = 512
KV_DIM = 320


EPSILON = 1e-05
ROPE_BASE = 100000.0
MASKED_SCORE = -1e30


def rms_scale(values):
    return lax.rsqrt(jnp.mean(values * values, axis=-1, keepdims=True) + EPSILON)


def frequencies():
    steps = jnp.arange(HEAD_DIM // 2, dtype=jnp.float32) * 2.0 / HEAD_DIM
    return ROPE_BASE ** (-steps)


def rotate(values, angles):
    middle = values.shape[-1] // 2
    cosines = jnp.cos(angles)[:, None, :]
    sines = jnp.sin(angles)[:, None, :]
    lower_half = values[..., :middle]
    upper_half = values[..., middle:]
    return jnp.concatenate(
        [lower_half * cosines - upper_half * sines, upper_half * cosines + lower_half * sines],
        axis=-1,
    )


def norm_backward(source, scale_rows, gain_vec, d_normed):
    normalized = source * scale_rows
    grad_gain = jnp.sum(d_normed * normalized, axis=0)
    weighted = d_normed * gain_vec
    d_source = scale_rows * (
        weighted - normalized * jnp.mean(weighted * normalized, axis=-1, keepdims=True)
    )
    return (d_source, grad_gain)


def block_scores(query_groups, key_block, key_offset, query_index, query_docs, token_docs):
    row_count = key_block.shape[0]
    raw = jnp.einsum("qhgd,khd->hgqk", query_groups, key_block, preferred_element_type=jnp.float32)
    key_index = key_offset + jnp.arange(row_count, dtype=jnp.int32)
    key_docs = lax.dynamic_slice_in_dim(token_docs, key_offset, row_count)
    allowed = (key_index[None, :] <= query_index[:, None]) & (
        key_docs[None, :] == query_docs[:, None]
    )
    return (raw * HEAD_DIM ** (-0.5), allowed[None, None])


def shards(
    tokens, cotangent, positions, doc_ids, gain_attn, w_qkv, w_out, gain_mlp, w_gate_up, w_down
):
    groups = HEADS // KV_HEADS
    seq_length = doc_ids.shape[1] * BLK
    row_start = lax.axis_index("ctx") * TOK_DEV
    query_index = row_start + jnp.arange(TOK_DEV, dtype=jnp.int32)
    token_docs = jnp.repeat(doc_ids[0], BLK)
    query_docs = lax.dynamic_slice_in_dim(token_docs, row_start, TOK_DEV)
    full_weights = (
        lax.all_gather(gain_attn, "fsdp", axis=0, tiled=True),
        lax.all_gather(w_qkv, "fsdp", axis=0, tiled=True),
        lax.all_gather(w_out, "fsdp", axis=0, tiled=True),
        lax.all_gather(gain_mlp, "fsdp", axis=0, tiled=True),
        lax.all_gather(w_gate_up, "fsdp", axis=0, tiled=True),
        lax.all_gather(w_down, "fsdp", axis=0, tiled=True),
    )
    gain_one, qkv_full, out_full, gain_two, gate_up_full, down_full = full_weights
    source = tokens[0].astype(jnp.float32)
    scale_attn = rms_scale(source)
    normed = (source * scale_attn * gain_one.astype(jnp.float32)).astype(jnp.bfloat16)
    mixed = jnp.dot(normed, qkv_full, preferred_element_type=jnp.float32)
    angles = positions[0].astype(jnp.float32)[:, None] * frequencies()[None, :]
    queries_b = rotate(mixed[:, :D].reshape(TOK_DEV, HEADS, HEAD_DIM), angles).astype(jnp.bfloat16)
    keys_rot = rotate(mixed[:, D : D + KV_DIM].reshape(TOK_DEV, KV_HEADS, HEAD_DIM), angles)
    key_value = jnp.concatenate(
        [keys_rot.reshape(TOK_DEV, KV_DIM), mixed[:, D + KV_DIM :]], axis=-1
    ).astype(jnp.bfloat16)
    query_groups = queries_b.reshape(TOK_DEV, KV_HEADS, groups, HEAD_DIM)
    start_state = (
        jnp.full((KV_HEADS, groups, TOK_DEV), MASKED_SCORE, jnp.float32),
        jnp.zeros((KV_HEADS, groups, TOK_DEV), jnp.float32),
        jnp.zeros((TOK_DEV, KV_HEADS, groups, HEAD_DIM), jnp.float32),
    )
    slab = lax.all_gather(key_value, "ctx", axis=0, tiled=True)
    block_total = slab.shape[0] // TOK_DEV
    slabs = slab.reshape(block_total, TOK_DEV, 2 * KV_DIM)
    offsets = TOK_DEV * jnp.arange(block_total, dtype=jnp.int32)

    def one_block(state, item):
        block_rows, key_offset = item
        best, totals, accum = state
        key_block = block_rows[:, :KV_DIM].reshape(TOK_DEV, KV_HEADS, HEAD_DIM)
        value_block = block_rows[:, KV_DIM:].reshape(TOK_DEV, KV_HEADS, HEAD_DIM)
        scores, allowed = block_scores(
            query_groups, key_block, key_offset, query_index, query_docs, token_docs
        )
        new_best = jnp.maximum(best, jnp.max(jnp.where(allowed, scores, MASKED_SCORE), axis=-1))
        expo = jnp.where(allowed, jnp.exp(scores - new_best[..., None]), 0.0)
        decay = jnp.exp(best - new_best)
        totals = totals * decay + jnp.sum(expo, axis=-1)
        added = jnp.einsum(
            "hgqk,khd->qhgd",
            expo.astype(jnp.bfloat16),
            value_block,
            preferred_element_type=jnp.float32,
        )
        accum = accum * jnp.transpose(decay, (2, 0, 1))[..., None] + added
        return ((new_best, totals, accum), None)

    best, totals, accum = lax.scan(one_block, start_state, (slabs, offsets))[0]
    attn_groups = accum / jnp.transpose(totals, (2, 0, 1))[..., None]
    log_total = best + jnp.log(totals)
    attended_b = attn_groups.reshape(TOK_DEV, D).astype(jnp.bfloat16)
    hidden = source + jnp.dot(attended_b, out_full, preferred_element_type=jnp.float32)
    scale_mlp = rms_scale(hidden)
    normed_mlp = (hidden * scale_mlp * gain_two.astype(jnp.float32)).astype(jnp.bfloat16)
    gate_up = jnp.dot(normed_mlp, gate_up_full, preferred_element_type=jnp.float32)
    gate_part = gate_up[:, :FF]
    up_part = gate_up[:, FF:]
    silu_gate = jax.nn.silu(gate_part)
    activated = (silu_gate * up_part).astype(jnp.bfloat16)
    result = hidden + jnp.dot(activated, down_full, preferred_element_type=jnp.float32)
    output = result.astype(jnp.bfloat16)[None]
    back_weights = (
        lax.all_gather(gain_attn, "fsdp", axis=0, tiled=True),
        lax.all_gather(w_qkv, "fsdp", axis=0, tiled=True),
        lax.all_gather(w_out, "fsdp", axis=0, tiled=True),
        lax.all_gather(gain_mlp, "fsdp", axis=0, tiled=True),
        lax.all_gather(w_gate_up, "fsdp", axis=0, tiled=True),
        lax.all_gather(w_down, "fsdp", axis=0, tiled=True),
    )
    gain_one, qkv_full, out_full, gain_two, gate_up_full, down_full = back_weights
    grad_out_b = cotangent[0]
    d_activated = jnp.dot(grad_out_b, down_full.T, preferred_element_type=jnp.float32)
    grad_down = jnp.dot(activated.T, grad_out_b, preferred_element_type=jnp.float32)
    sigmoid_gate = jax.nn.sigmoid(gate_part)
    d_gate = d_activated * up_part * sigmoid_gate * (1.0 + gate_part * (1.0 - sigmoid_gate))
    d_up = d_activated * silu_gate
    d_gate_up = jnp.concatenate([d_gate, d_up], axis=-1).astype(jnp.bfloat16)
    grad_gate_up = jnp.dot(normed_mlp.T, d_gate_up, preferred_element_type=jnp.float32)
    d_normed_mlp = jnp.dot(d_gate_up, gate_up_full.T, preferred_element_type=jnp.float32)
    d_from_norm, grad_gain_mlp = norm_backward(
        hidden, scale_mlp, gain_two.astype(jnp.float32), d_normed_mlp
    )
    d_hidden = grad_out_b.astype(jnp.float32) + d_from_norm
    d_hidden_b = d_hidden.astype(jnp.bfloat16)
    grad_out_proj = jnp.dot(attended_b.T, d_hidden_b, preferred_element_type=jnp.float32)
    d_attended = jnp.dot(d_hidden_b, out_full.T, preferred_element_type=jnp.float32).astype(
        jnp.bfloat16
    )
    d_out_groups = d_attended.reshape(TOK_DEV, KV_HEADS, groups, HEAD_DIM)
    row_delta = jnp.transpose(
        jnp.sum(d_out_groups.astype(jnp.float32) * attn_groups, axis=-1), (1, 2, 0)
    )
    key_value_all = lax.all_gather(key_value, "ctx", axis=0, tiled=True)
    block_total = seq_length // TOK_DEV
    all_slabs = key_value_all.reshape(block_total, TOK_DEV, 2 * KV_DIM)
    all_offsets = TOK_DEV * jnp.arange(block_total, dtype=jnp.int32)

    def back_block(d_query, item):
        block_rows, key_offset = item
        key_block = block_rows[:, :KV_DIM].reshape(TOK_DEV, KV_HEADS, HEAD_DIM)
        value_block = block_rows[:, KV_DIM:].reshape(TOK_DEV, KV_HEADS, HEAD_DIM)
        scores, allowed = block_scores(
            query_groups, key_block, key_offset, query_index, query_docs, token_docs
        )
        probability = jnp.where(allowed, jnp.exp(scores - log_total[..., None]), 0.0)
        d_value = jnp.einsum(
            "hgqk,qhgd->khd",
            probability.astype(jnp.bfloat16),
            d_out_groups,
            preferred_element_type=jnp.float32,
        )
        d_prob = jnp.einsum(
            "qhgd,khd->hgqk", d_out_groups, value_block, preferred_element_type=jnp.float32
        )
        d_scores = (probability * (d_prob - row_delta[..., None])).astype(jnp.bfloat16)
        d_query = d_query + HEAD_DIM ** (-0.5) * jnp.einsum(
            "hgqk,khd->qhgd", d_scores, key_block, preferred_element_type=jnp.float32
        )
        d_key = HEAD_DIM ** (-0.5) * jnp.einsum(
            "hgqk,qhgd->khd", d_scores, query_groups, preferred_element_type=jnp.float32
        )
        return (
            d_query,
            jnp.concatenate(
                [d_key.reshape(TOK_DEV, KV_DIM), d_value.reshape(TOK_DEV, KV_DIM)], axis=-1
            ),
        )

    d_query_zero = jnp.zeros((TOK_DEV, KV_HEADS, groups, HEAD_DIM), jnp.float32)
    d_query, key_terms = lax.scan(back_block, d_query_zero, (all_slabs, all_offsets))
    key_grads = lax.psum_scatter(
        key_terms.reshape(seq_length, 2 * KV_DIM).astype(jnp.bfloat16),
        "ctx",
        scatter_dimension=0,
        tiled=True,
    ).astype(jnp.float32)
    d_queries = rotate(d_query.reshape(TOK_DEV, HEADS, HEAD_DIM), -angles).reshape(TOK_DEV, D)
    d_keys = rotate(key_grads[:, :KV_DIM].reshape(TOK_DEV, KV_HEADS, HEAD_DIM), -angles).reshape(
        TOK_DEV, KV_DIM
    )
    d_mixed = jnp.concatenate([d_queries, d_keys, key_grads[:, KV_DIM:]], axis=-1).astype(
        jnp.bfloat16
    )
    grad_qkv = jnp.dot(normed.T, d_mixed, preferred_element_type=jnp.float32)
    d_normed = jnp.dot(d_mixed, qkv_full.T, preferred_element_type=jnp.float32)
    d_source, grad_gain_attn = norm_backward(
        source, scale_attn, gain_one.astype(jnp.float32), d_normed
    )
    input_grad = (d_hidden + d_source).astype(jnp.bfloat16)[None]
    owned = (
        lax.psum_scatter(
            grad_gain_attn.astype(jnp.bfloat16), "fsdp", scatter_dimension=0, tiled=True
        ).astype(jnp.float32),
        lax.psum_scatter(
            grad_qkv.astype(jnp.bfloat16), "fsdp", scatter_dimension=0, tiled=True
        ).astype(jnp.float32),
        lax.psum_scatter(
            grad_out_proj.astype(jnp.bfloat16), "fsdp", scatter_dimension=0, tiled=True
        ).astype(jnp.float32),
        lax.psum_scatter(
            grad_gain_mlp.astype(jnp.bfloat16), "fsdp", scatter_dimension=0, tiled=True
        ).astype(jnp.float32),
        lax.psum_scatter(
            grad_gate_up.astype(jnp.bfloat16), "fsdp", scatter_dimension=0, tiled=True
        ).astype(jnp.float32),
        lax.psum_scatter(
            grad_down.astype(jnp.bfloat16), "fsdp", scatter_dimension=0, tiled=True
        ).astype(jnp.float32),
    )
    summed = (
        lax.psum(owned[0].astype(jnp.bfloat16), ("seq", "ctx")).astype(jnp.float32),
        lax.psum(owned[1].astype(jnp.bfloat16), ("seq", "ctx")).astype(jnp.float32),
        lax.psum(owned[2].astype(jnp.bfloat16), ("seq", "ctx")).astype(jnp.float32),
        lax.psum(owned[3].astype(jnp.bfloat16), ("seq", "ctx")).astype(jnp.float32),
        lax.psum(owned[4].astype(jnp.bfloat16), ("seq", "ctx")).astype(jnp.float32),
        lax.psum(owned[5].astype(jnp.bfloat16), ("seq", "ctx")).astype(jnp.float32),
    )
    return (output, input_grad, summed[0], summed[1], summed[2], summed[3], summed[4], summed[5])


def solution(mesh):
    placed = (
        P(("seq", "fsdp"), "ctx", None),
        P(("seq", "fsdp"), "ctx", None),
        P(("seq", "fsdp"), "ctx"),
        P(("seq", "fsdp"), None),
        P("fsdp"),
        P("fsdp", None),
        P("fsdp", None),
        P("fsdp"),
        P("fsdp", None),
        P("fsdp", None),
    )
    return jax.shard_map(
        shards,
        mesh=mesh,
        in_specs=placed,
        out_specs=(
            P(("seq", "fsdp"), "ctx", None),
            P(("seq", "fsdp"), "ctx", None),
            P("fsdp"),
            P("fsdp", None),
            P("fsdp", None),
            P("fsdp"),
            P("fsdp", None),
            P("fsdp", None),
        ),
        check_vma=False,
    )
```

profile of v0, /device:TPU:0, one launch (start us, length us, event | category | flops | bytes accessed | tf_op | source)
XLA Modules:
  0.0 1027.2 jit_solution(8336753694661807820)
XLA Ops:
  12.4 13.6 %all-reduce.7 = (bf16[960]{0:T(1024)(128)(2,1)S(1)}, bf16[960]{0:T(1024)(128)(2,1)S(1)}) all-reduce(bf16[960]{0:T(1024)(128)(2,1)S(1)} %dynamic-update-slice, bf16[960]{0:T(1024)(128)(2,1)S(1)} %dynamic-update-slice.1), channel_id=1, replica_groups=mesh['seq'=4,'ctx'=2,'fsdp'=4] {'fsdp'}, use_global_device_ids=true, to_apply=%add | all-reduce | flops 1920 | bytes 7680
  28.8 47.9 %all-gather.6.cloned.1.call-done = bf16[960,1600]{1,0:T(8,128)(2,1)} async-done(((bf16[240,1600]{1,0:T(8,128)(2,1)}), bf16[960,1600]{1,0:T(8,128)(2,1)}) %all-gather.6.cloned.1.call-update) | async-done | bytes 3072016 | tf_op jit(solution)/shard_map/all_gather | solution.py:74
  88.0 18.8 %all-gather.8.cloned.1.call-done = bf16[1024,640]{0,1:T(8,128)(2,1)} async-done(((bf16[512,640]{0,1:T(8,128)(2,1)}), bf16[1024,640]{0,1:T(8,128)(2,1)}) %all-gather.8.cloned.1.call-update) | async-done | bytes 1310736 | tf_op jit(solution)/shard_map/all_gather | solution.py:97
  109.3 60.7 %while.28 = (s32[]{:T(128)}, f32[5,3,512]{2,1,0:T(4,128)S(1)}, f32[5,3,512]{2,1,0:T(4,128)S(1)}, f32[512,5,3,64]{0,3,2,1:T(8,128)}, s32[2]{0:T(128)S(1)}, /*inde...) while((s32[]{:T(128)}, f32[5,3,512]{2,1,0:T(4,128)S(1)}, ...), condition=%wide.region_4.5_spmd.clone, body=%wide.region_1.4_spmd.clone.sunk | while | flops 1052194816 | bytes 56934604 | solution.py:123
  120.9 8.8 fusion.122
  129.7 8.7 bitcast_add_fusion.4
  150.1 8.7 fusion.122
  158.8 11.1 %bitcast_add_fusion.4 = f32[512,5,3,64]{0,3,2,1:T(8,128)} fusion(f32[512,5,3,64]{0,3,2,1:T(8,128)} %get-tuple-element.585, bf16[512,5,64,1]{0,2,3,1:T(8,128)(2,1)S(1)} %bitcast.226, f32[5,512,512,3]{2,1,3,0:T(8,128)} %get-tuple-element.550, f32[5,3,512]{2,1,0:T(4,128)S(1)} %get-tuple-element.596, pred[512,512]{0,1:T(8,128)(4,1)S(1)} %compare_and_fusion.4, ...), kind=kOutput, calls=%fused_computation.11.clone.1 | convolution fusion | flops 520519680 | bytes 20312064 | tf_op jit(solution)/shard_map/while/body/eval_jaxpr/hgqk,khd->qhgd/dot_general | solution.py:114
  177.5 148.0 %all-gather.12.cloned.1.call-done = bf16[960,5120]{1,0:T(8,128)(2,1)} async-done(((bf16[240,5120]{1,0:T(8,128)(2,1)}), bf16[960,5120]{1,0:T(8,128)(2,1)}) %all-gather.12.cloned.1.call-update) | async-done | bytes 9830416 | tf_op jit(solution)/shard_map/all_gather | solution.py:77
  325.5 11.4 %fusion.61 = f32[512,5120]{1,0:T(8,128)} fusion(bf16[960,5120]{1,0:T(8,128)(2,1)} %all-gather.12.cloned.1.call-done, f32[512,960]{0,1:T(8,128)} %get-tuple-element.408, f32[960]{0:T(1024)S(1)} %convert_element_type.134, f32[512]{0:T(512)S(1)} %add_rsqrt_fusion), kind=kOutput, calls=%fused_computation.122 | convolution fusion | flops 5034639360 | bytes 22288128 | tf_op jit(solution)/shard_map/dot_general | solution.py:130
  336.9 80.9 %all-gather.14.cloned.1.call-done = bf16[2560,960]{0,1:T(8,128)(2,1)} async-done(((bf16[640,960]{0,1:T(8,128)(2,1)}), bf16[2560,960]{0,1:T(8,128)(2,1)}) %all-gather.14.cloned.1.call-update) | async-done | bytes 4915216 | tf_op jit(solution)/shard_map/all_gather | solution.py:78
  417.8 10.7 %multiply_convert_fusion.1 = (bf16[512,2560]{1,0:T(8,128)(2,1)S(1)}, bf16[512,2560]{1,0:T(8,128)(2,1)S(1)}, bf16[512,2560]{1,0:T(8,128)(2,1)}) fusion(f32[512,5120]{1,0:T(8,128)} %fusion.61, bf16[2560,960]{0,1:T(8,128)(2,1)} %all-gather.14.cloned.1.call-done, bf16[1,512,960]{1,2,0:T(8,128)(2,1)} %param.15), kind=kOutput, calls=%fused_computation.48 | convolution fusion | flops 2536243200 | bytes 24248320 | tf_op jit(solution)/shard_map/dot_general | solution.py:147
  439.0 78.2 %while.29 = (s32[]{:T(128)}, f32[512,5,3,64]{0,3,2,1:T(8,128)S(1)}, bf16[2,512,640]{2,1,0:T(8,128)(2,1)}, bf16[2,512,640]{1,2,0:T(8,128)(2,1)}, s32[2]{0:T(128)S...) while((s32[]{:T(128)}, f32[512,5,3,64]{0,3,2,1:T(8,128)S(1)}, ...), condition=%wide.region_9.10_spmd.clone, body=%wide.region_8.9_spmd.clone.sunk | while | flops 2559804416 | bytes 87730400 | solution.py:205
  451.8 8.8 fusion.137
  460.6 8.6 fusion.136
  490.7 8.8 fusion.137
  548.7 11.5 %convolution_convert_fusion = bf16[960,5120]{1,0:T(8,128)(2,1)} fusion(bf16[512,2560]{1,0:T(8,128)(2,1)} %copy-done.35, bf16[512,2560]{1,0:T(8,128)(2,1)} %copy-done.34, f32[512,960]{0,1:T(8,128)S(1)} %copy-done.4, f32[960]{0:T(1024)S(1)} %copy-done.22, f32[512]{0:T(512)S(1)} %copy-done.26), kind=kOutput, calls=%fused_computation.44 | convolution fusion | flops 5050040320 | bytes 17045248 | tf_op jit(solution)/shard_map/dot_general | solution.py:153
  560.3 77.4 %reduce-scatter.16.cloned.1.call-done = bf16[640,960]{1,0:T(8,128)(2,1)} async-done(((bf16[2560,960]{1,0:T(8,128)(2,1)}), bf16[640,960]{1,0:T(8,128)(2,1)}) %reduce-scatter.16.cloned.1.call-update) | async-done | bytes 1228816
  640.0 42.6 %reduce-scatter.12.cloned.1.call-done = bf16[240,960]{1,0:T(8,128)(2,1)} async-done(((bf16[960,960]{1,0:T(8,128)(2,1)}), bf16[240,960]{1,0:T(8,128)(2,1)}) %reduce-scatter.12.cloned.1.call-update) | async-done | bytes 460816 | tf_op jit(solution)/shard_map/reduce_scatter | solution.py:232
  682.6 63.5 %reduce-scatter.10.cloned.1.call-done = bf16[240,1600]{1,0:T(8,128)(2,1)} async-done(((bf16[960,1600]{1,0:T(8,128)(2,1)}), bf16[240,1600]{1,0:T(8,128)(2,1)}) %reduce-scatter.10.cloned.1.call-update) | async-done | bytes 768016 | tf_op jit(solution)/shard_map/reduce_scatter | solution.py:229
  746.1 169.9 %reduce-scatter.14.cloned.1.call-done = bf16[240,5120]{1,0:T(8,128)(2,1)} async-done(((bf16[960,5120]{1,0:T(8,128)(2,1)}), bf16[240,5120]{1,0:T(8,128)(2,1)}) %reduce-scatter.14.cloned.1.call-update) | async-done | bytes 2457616 | tf_op jit(solution)/shard_map/reduce_scatter | solution.py:238
  927.2 11.4 %all-reduce.6 = (bf16[960]{0:T(1024)(128)(2,1)S(1)}, bf16[960]{0:T(1024)(128)(2,1)S(1)}) all-reduce(bf16[960]{0:T(1024)(128)(2,1)S(1)} %get-tuple-element.320, bf16[960]{0:T(1024)(128)(2,1)S(1)} %copy-done.31), channel_id=3, replica_groups=mesh['seq'=4,'ctx'=2,'fsdp'=4] {'fsdp'}, use_global_device_ids=true, to_apply=%region_13.14.clone | all-reduce | flops 1920 | bytes 7680
  938.7 14.2 %all-reduce.4 = (bf16[240]{0:T(256)(128)(2,1)S(1)}, bf16[240]{0:T(256)(128)(2,1)S(1)}) all-reduce(bf16[240]{0:T(256)(128)(2,1)S(1)} %dynamic-slice.3, bf16[240]{0:T(256)(128)(2,1)S(1)} %dynamic-slice.5), channel_id=1, replica_groups=mesh['seq'=4,'ctx'=2,'fsdp'=4] {'seq','ctx'}, use_global_device_ids=true, to_apply=%region_14.15 | all-reduce | flops 480 | bytes 1920 | tf_op jit(solution)/shard_map/psum | solution.py:246
  957.1 55.4 %all-reduce.10.cloned.1.call-done = (bf16[240,1600]{1,0:T(8,128)(2,1)}, bf16[240,960]{1,0:T(8,128)(2,1)}, bf16[240,5120]{1,0:T(8,128)(2,1)}, bf16[640,960]{0,1:T(8,128)(2,1)}) async-done(((bf16[240,1600]{1,0:T(8,128)(2,1)}, bf16[240,960]{1,0:T(8,128)(2,1)}, bf16[240,5120]{1,0:T(8,128)(2,1)}, bf16[640,960]{0,1:T(8,128)(2,1)}), (bf16[240,1600]{1,0:T(8,128)(2,1)}, bf16[240,960]{1,0:T(8,128)(2,1)}, ...) | async-done | bytes 4915216 | tf_op jit(solution)/shard_map/psum | solution.py:247
  (205 shorter events, 162.4 us)
Async XLA Ops:
  7.2 78.8 %copy-start = (s32[1,8]{1,0:T(1,128)S(1)}, s32[1,8]{1,0:T(1,128)}, u32[]{:S(2)}) copy-start(s32[1,8]{1,0:T(1,128)} %param.17) | copy-start | bytes 100
  7.2 69.5 %all-gather.6.cloned.1.call-start = ((), (), s32[]{:S(2)}) async-start(), calls=%async_computation.5 | async-start | bytes 3993600 | tf_op jit(solution)/shard_map/all_gather | solution.py:74
  7.9 98.9 %all-gather.8.cloned.1.call-start = ((), (), s32[]{:S(2)}) async-start(), calls=%async_computation.6 | async-start | bytes 1966080 | tf_op jit(solution)/shard_map/all_gather | solution.py:97
  26.1 54.9 %copy-start.27 = (f32[960]{0:T(1024)}, f32[960]{0:T(1024)S(1)}, u32[]{:S(2)}) copy-start(f32[960]{0:T(1024)S(1)} %convert_element_type.128) | copy-start | bytes 11524
  27.5 53.4 %copy-start.29 = (f32[512]{0:T(512)}, f32[512]{0:T(512)S(1)}, u32[]{:S(2)}) copy-start(f32[512]{0:T(512)S(1)} %add_rsqrt_fusion.1) | copy-start | bytes 6148
  83.8 89.0 %all-gather.10.cloned.1.call-start = ((), (), s32[]{:S(2)}) async-start(), calls=%async_computation.7 | async-start | bytes 2457600 | tf_op jit(solution)/shard_map/all_gather | solution.py:75
  84.5 241.0 %all-gather.12.cloned.1.call-start = ((), (), s32[]{:S(2)}) async-start(), calls=%async_computation.8 | async-start | bytes 12288000 | tf_op jit(solution)/shard_map/all_gather | solution.py:77
  85.1 332.7 %all-gather.14.cloned.1.call-start = ((), (), s32[]{:S(2)}) async-start(), calls=%async_computation.9 | async-start | bytes 6144000 | tf_op jit(solution)/shard_map/all_gather | solution.py:78
  85.7 455.7 %reduce-scatter.8.cloned.1.call-start = ((), (), s32[]{:S(2)}) async-start(), calls=%async_computation.10 | async-start | bytes 1966080 | tf_op jit(solution)/shard_map/reduce_scatter | solution.py:206
  86.0 348.7 %copy-start.21 = (f32[960]{0:T(1024)}, f32[960]{0:T(1024)S(1)}, u32[]{:S(2)}) copy-start(f32[960]{0:T(1024)S(1)} %convert_element_type.134) | copy-start | bytes 11524
  177.5 257.2 %copy-start.25 = (f32[512]{0:T(512)}, f32[512]{0:T(512)S(1)}, u32[]{:S(2)}) copy-start(f32[512]{0:T(512)S(1)} %add_rsqrt_fusion) | copy-start | bytes 6148
  417.8 10.7 %copy-start.2 = (bf16[960,5120]{1,0:T(8,128)(2,1)S(1)}, bf16[960,5120]{1,0:T(8,128)(2,1)}, u32[]{:S(2)}) copy-start(bf16[960,5120]{1,0:T(8,128)(2,1)} %all-gather.12.cloned.1.call-done) | copy-start | bytes 29491204
  417.8 10.7 %copy-start.3 = (f32[512,960]{0,1:T(8,128)S(1)}, f32[512,960]{0,1:T(8,128)}, u32[]{:S(2)}) copy-start(f32[512,960]{0,1:T(8,128)} %get-tuple-element.408) | copy-start | bytes 5898244
  428.6 6.1 copy-start.35
  428.6 6.1 copy-start.12
  519.7 118.0 %reduce-scatter.16.cloned.1.call-start = ((), (), s32[]{:S(2)}) async-start(), calls=%async_computation.14 | async-start | bytes 6553600
  533.8 148.9 %reduce-scatter.12.cloned.1.call-start = ((), (), s32[]{:S(2)}) async-start(), calls=%async_computation.12 | async-start | bytes 2457600 | tf_op jit(solution)/shard_map/reduce_scatter | solution.py:232
  539.0 207.1 %reduce-scatter.10.cloned.1.call-start = ((), (), s32[]{:S(2)}) async-start(), calls=%async_computation.11 | async-start | bytes 3993600 | tf_op jit(solution)/shard_map/reduce_scatter | solution.py:229
  547.2 368.7 %reduce-scatter.14.cloned.1.call-start = ((), (), s32[]{:S(2)}) async-start(), calls=%async_computation.13 | async-start | bytes 12288000 | tf_op jit(solution)/shard_map/reduce_scatter | solution.py:238
  560.2 452.3 %all-reduce.10.cloned.1.call-start = ((), (), s32[]{:S(2)}) async-start(), calls=%async_computation.15 | async-start | bytes 9953280 | tf_op jit(solution)/shard_map/psum | solution.py:247
  916.7 7.1 copy-start.17
  916.7 7.1 copy-start.24
  916.7 7.1 copy-start.32
  923.8 30.3 %copy-start.8 = (f32[512,960]{0,1:T(8,128)S(1)}, f32[512,960]{0,1:T(8,128)}, u32[]{:S(2)}) copy-start(f32[512,960]{0,1:T(8,128)} %copy-done.7) | copy-start | bytes 5898244
  (24 other events, 65.9 us)
Sparse Core Ops, SparseCore 0:
  9.6 67.0 all-gather.5
  83.9 22.8 all-gather.7
  108.4 43.5 all-gather.9
  153.4 172.0 all-gather.11
  326.9 90.8 all-gather.13
  519.8 21.5 reduce-scatter.7
  543.8 93.7 reduce-scatter.15
  640.6 41.9 reduce-scatter.11
  685.6 60.4 reduce-scatter.9
  748.3 167.6 reduce-scatter.13
  920.7 91.6 all-reduce.9
where the time goes:
time: 1030 us
  waiting for transfers between devices  709 us (69%)
  matrix products  166 us (16%)
  other arithmetic  44.4 us (4%)
  local copies, waits for them, and re-layouts  44 us (4%)
  blocking collectives  39.2 us (4%)
  between operations  15.9 us (2%)
    reduce_scatter x1, waiting for transfers between devices, shards(): lax.psum_scatter(grad_gate_up.astype(jnp.bfloat16), 'fsdp', scatter_dimen...  170 us
    all_gather x1, waiting for transfers between devices, shards(): lax.all_gather(w_gate_up, 'fsdp', axis=0, tiled=True)  148 us
    all_gather x1, waiting for transfers between devices, shards(): lax.all_gather(w_down, 'fsdp', axis=0, tiled=True)  80.9 us
    unnamed x12, waiting for transfers between devices  79.9 us
    reduce_scatter x1, waiting for transfers between devices, shards(): lax.psum_scatter(grad_qkv.astype(jnp.bfloat16), 'fsdp', scatter_dimension...  63.5 us
    psum x1, waiting for transfers between devices, shards(): lax.psum(owned[1].astype(jnp.bfloat16), ('seq', 'ctx')).astype(jnp.float32)  55.4 us
    all_gather x1, waiting for transfers between devices, shards(): lax.all_gather(w_qkv, 'fsdp', axis=0, tiled=True)  47.9 us
    reduce_scatter x1, waiting for transfers between devices, shards(): lax.psum_scatter(grad_out_proj.astype(jnp.bfloat16), 'fsdp', scatter_dime...  42.6 us
  transfers between devices with their start and end apart: 11, of which 10 were waited for; matrix products, arithmetic and copies ran while one was open for 13% of the time, Pallas kernels for 0%

commit v1 on v0

--- a/solution.py
+++ b/solution.py
@@ -1,6 +1,10 @@
+import functools
+
 import jax
 import jax.numpy as jnp
 from jax import lax
+from jax.experimental import pallas as pl
+from jax.experimental.pallas import tpu as pltpu
 from jax.sharding import PartitionSpec as P
 
 D = 960
@@ -11,11 +15,25 @@
 BLK = 128
 TOK_DEV = 512
 KV_DIM = 320
-
+QKV = D + 2 * KV_DIM
+FF_HALF = FF // 2
+FF_SHARD = FF // 4
+ROWS = D // 4
+ROWS_PAD = 256
+SLICE = 32
+CHUNKS = ((0, 256), (256, 384))
+ROW_TILE = 256
+VMEM_LIMIT = 56 * 1024 * 1024
 
 EPSILON = 1e-05
 ROPE_BASE = 100000.0
 MASKED_SCORE = -1e30
+AXES = ("seq", "ctx", "fsdp")
+F32 = jnp.float32
+BF16 = jnp.bfloat16
+ANY = pl.BlockSpec(memory_space=pl.ANY)
+SMEM = pl.BlockSpec(memory_space=pltpu.SMEM)
+VMEM = pl.BlockSpec(memory_space=pltpu.VMEM)
 
 
 def rms_scale(values):
@@ -49,6 +67,403 @@
     return (d_source, grad_gain)
 
 
+def after(value, *earlier):
+    return lax.optimization_barrier((value, *earlier))[0]
+
+
+class Links:
+    def __init__(self, sizes):
+        self.sizes = sizes
+
+    def index(self, s, c, f):
+        return (s * self.sizes[1] + c) * self.sizes[2] + f
+
+    def swap(self, value, ds=0, dc=0, df=0, only=None):
+        n_s, n_c, n_f = self.sizes
+        pairs = [
+            (self.index(s, c, f), self.index(s ^ ds, c ^ dc, f ^ df))
+            for s in range(n_s)
+            for c in range(n_c)
+            for f in range(n_f)
+            if only is None or only(s, f)
+        ]
+        return lax.ppermute(value, AXES, pairs)
+
+    def core(self, value):
+        return self.swap(value, ds=1)
+
+    def plane(self, value, bits):
+        return self.swap(value, ds=bits & 2, dc=bits & 1)
+
+    def gather_plane(self, own, first=None):
+        if first is None:
+            return [own] + [self.plane(own, bits) for bits in (1, 2, 3)]
+        second = 3 - first
+        pieces = [own, None, None, None]
+        pieces[first] = self.plane(own, first)
+        pieces[second] = self.plane(own, second)
+        pieces[3] = self.plane(pieces[first], second)
+        return pieces
+
+    def gather_z(self, own):
+        return jnp.stack([self.swap(own, df=bits) for bits in (1, 2, 3)])
+
+    def reduce_plane(self, pieces, first):
+        second = 3 - first
+        far = self.plane(pieces[3], first)
+        near = self.plane(pieces[first], first)
+        forward = (pieces[second].astype(F32) + far.astype(F32)).astype(BF16)
+        last = self.plane(forward, second)
+        total = pieces[0].astype(F32) + near.astype(F32) + last.astype(F32)
+        total = total.astype(BF16)
+        step = 2
+        while step < self.sizes[1]:
+            total = (total.astype(F32) + self.swap(total, dc=step).astype(F32)).astype(BF16)
+            step *= 2
+        return total
+
+    def reduce_z(self, total):
+        arrived = [self.swap(total[bits], df=bits) for bits in (1, 2, 3)]
+        result = total[0].astype(F32)
+        for value in arrived:
+            result = result + value.astype(F32)
+        return result.astype(BF16)
+
+
+def assemble_rows_kernel(place, own, m0, m1, m2, m3, t0, t1, t2, t3, full, sem):
+    p, k, f = place[0], place[1], place[2]
+    first = pltpu.make_async_copy(own, full.at[f], sem)
+    first.start()
+    first.wait()
+    for start in (True, False):
+        for other, refs in enumerate(((m0, m1, m2, m3), (t0, t1, t2, t3))):
+            kk = jnp.bitwise_xor(k, other)
+            for q, ref in enumerate(refs):
+                pp = jnp.bitwise_xor(p, q)
+                row = pl.multiple_of(kk * 128 + pp * SLICE, 16)
+                short = (kk * 4 + pp) == 7
+                for r in range(3):
+                    z = jnp.bitwise_xor(f, r + 1)
+
+                    def go(count, ref=ref, r=r, z=z, row=row):
+                        copy = pltpu.make_async_copy(
+                            ref.at[r, pl.ds(0, count)], full.at[z, pl.ds(row, count)], sem
+                        )
+                        if start:
+                            copy.start()
+                        else:
+                            copy.wait()
+
+                    pl.when(short)(functools.partial(go, 16))
+                    pl.when(jnp.logical_not(short))(functools.partial(go, SLICE))
+
+
+def assemble_rows(place, own, mine, theirs):
+    width = own.shape[1]
+    return pl.pallas_call(
+        assemble_rows_kernel,
+        out_shape=jax.ShapeDtypeStruct((4, ROWS, width), BF16),
+        in_specs=[SMEM] + [ANY] * 9,
+        out_specs=VMEM,
+        scratch_shapes=[pltpu.SemaphoreType.DMA(())],
+        compiler_params=pltpu.CompilerParams(vmem_limit_bytes=VMEM_LIMIT),
+        cost_estimate=pl.CostEstimate(flops=0, bytes_accessed=4 * D * width, transcendentals=0),
+    )(place, own, *mine, *theirs).reshape(D, width)
+
+
+def scatter_rows_kernel(place, grad, m0, m1, m2, m3, t0, t1, t2, t3, sem):
+    p, k, f = place[0], place[1], place[2]
+    for start in (True, False):
+        for other, refs in enumerate(((m0, m1, m2, m3), (t0, t1, t2, t3))):
+            kk = jnp.bitwise_xor(k, other)
+            for q, ref in enumerate(refs):
+                pp = jnp.bitwise_xor(p, q)
+                row = pl.multiple_of(kk * 128 + pp * SLICE, 16)
+                short = (kk * 4 + pp) == 7
+                for r in range(4):
+                    z = jnp.bitwise_xor(f, r)
+
+                    def go(count, ref=ref, r=r, z=z, row=row):
+                        copy = pltpu.make_async_copy(
+                            grad.at[z, pl.ds(row, count)], ref.at[r, pl.ds(0, count)], sem
+                        )
+                        if start:
+                            copy.start()
+                        else:
+                            copy.wait()
+
+                    pl.when(short)(functools.partial(go, 16))
+                    pl.when(jnp.logical_not(short))(functools.partial(go, SLICE))
+
+
+def scatter_rows(place, grad):
+    width = grad.shape[1]
+    piece = jax.ShapeDtypeStruct((4, SLICE, width), BF16)
+    out = pl.pallas_call(
+        scatter_rows_kernel,
+        out_shape=[piece] * 8,
+        in_specs=[SMEM, VMEM],
+        out_specs=[ANY] * 8,
+        scratch_shapes=[pltpu.SemaphoreType.DMA(())],
+        compiler_params=pltpu.CompilerParams(vmem_limit_bytes=VMEM_LIMIT),
+        cost_estimate=pl.CostEstimate(flops=0, bytes_accessed=4 * D * width, transcendentals=0),
+    )(place, grad.reshape(4, ROWS, width))
+    return out[:4], out[4:]
+
+
+def finish_rows_kernel(place, m0, m1, m2, m3, t0, t1, t2, t3, full):
+    p, k = place[0], place[1]
+    for other, refs in enumerate(((m0, m1, m2, m3), (t0, t1, t2, t3))):
+        kk = jnp.bitwise_xor(k, other)
+        for q, ref in enumerate(refs):
+            pp = jnp.bitwise_xor(p, q)
+            row = pl.multiple_of(kk * 128 + pp * SLICE, 16)
+            short = (kk * 4 + pp) == 7
+
+            def go(count, ref=ref, row=row):
+                full[pl.ds(row, count), :] = ref[pl.ds(0, count), :].astype(F32)
+
+            pl.when(short)(functools.partial(go, 16))
+            pl.when(jnp.logical_not(short))(functools.partial(go, SLICE))
+
+
+def finish_rows(place, mine, theirs):
+    width = mine[0].shape[1]
+    return pl.pallas_call(
+        finish_rows_kernel,
+        out_shape=jax.ShapeDtypeStruct((ROWS, width), F32),
+        in_specs=[SMEM] + [VMEM] * 8,
+        out_specs=VMEM,
+        cost_estimate=pl.CostEstimate(flops=0, bytes_accessed=6 * ROWS * width, transcendentals=0),
+    )(place, *mine, *theirs)
+
+
+def rows_in(rows):
+    return (((0,), (0,)), ((), ()))
+
+
+NT = (((1,), (1,)), ((), ()))
+TN = (((0,), (0,)), ((), ()))
+
+
+def mlp_kernel(
+    first,
+    last,
+    start_col,
+    place,
+    x_own,
+    x_oth,
+    dy_own,
+    dy_oth,
+    gate_up_own,
+    u0,
+    u1,
+    u2,
+    u3,
+    d0,
+    d1,
+    d2,
+    d3,
+    *rest,
+):
+    if first:
+        carried = None
+    else:
+        carried, rest = rest[:4], rest[4:]
+    out_own, out_oth, dn_own, dn_oth = rest[:4]
+    gu_out = rest[4:8]
+    gd_out = rest[8:12]
+    up_w, down_w, act, dgu, gu, gd, x, dy, acc_out, acc_dn, sem = rest[12:]
+    width = act.shape[1]
+    p, k, f = place[0], place[1], place[2]
+
+    copies = []
+    for half, (xs, ds) in enumerate(((x_own, dy_own), (x_oth, dy_oth))):
+        rows = pl.ds(half * TOK_DEV, TOK_DEV)
+        copies.append(pltpu.make_async_copy(xs, x.at[rows], sem))
+        copies.append(pltpu.make_async_copy(ds, dy.at[rows], sem))
+    for pp in range(4):
+        col = pl.multiple_of((pp // 2) * FF + k * FF_HALF + (pp % 2) * FF_SHARD + start_col, 128)
+        copies.append(
+            pltpu.make_async_copy(gate_up_own.at[:, pl.ds(col, width)], up_w.at[pp, f], sem)
+        )
+    for q, ref in enumerate((u0, u1, u2, u3)):
+        for r in range(3):
+            copies.append(
+                pltpu.make_async_copy(
+                    ref.at[r], up_w.at[jnp.bitwise_xor(p, q), jnp.bitwise_xor(f, r + 1)], sem
+                )
+            )
+    for q, ref in enumerate((d0, d1, d2, d3)):
+        for t in range(2):
+            block = jnp.bitwise_xor(jnp.bitwise_and(f, 1), t)
+            copies.append(
+                pltpu.make_async_copy(ref.at[t], down_w.at[block, jnp.bitwise_xor(p, q)], sem)
+            )
+    if not first:
+        for half in range(2):
+            rows = pl.ds(half * TOK_DEV, TOK_DEV)
+            copies.append(pltpu.make_async_copy(carried[half], acc_out.at[rows], sem))
+            copies.append(pltpu.make_async_copy(carried[2 + half], acc_dn.at[rows], sem))
+    for copy in copies:
+        copy.start()
+    for copy in copies:
+        copy.wait()
+
+    for block in range(2):
+        gate_w = up_w[block].reshape(D, width)
+        lift_w = up_w[2 + block].reshape(D, width)
+        drop_w = down_w[block].reshape(width, D)
+
+        @pl.loop(0, 2 * TOK_DEV // ROW_TILE)
+        def tile(t):
+            rows = pl.ds(pl.multiple_of(t * ROW_TILE, ROW_TILE), ROW_TILE)
+            g = jnp.dot(x[rows, :], gate_w, preferred_element_type=F32)
+            u = jnp.dot(x[rows, :], lift_w, preferred_element_type=F32)
+            da = lax.dot_general(dy[rows, :], drop_w, NT, preferred_element_type=F32)
+            sig = jax.nn.sigmoid(g)
+            silu = g * sig
+            a = (silu * u).astype(BF16)
+            dg = (da * u * sig * (1.0 + g * (1.0 - sig))).astype(BF16)
+            du = (da * silu).astype(BF16)
+            act[rows, :] = a
+            dgu[rows, :width] = dg
+            dgu[rows, width:] = du
+            out = jnp.dot(a, drop_w, preferred_element_type=F32)
+            dn = lax.dot_general(dg, gate_w, NT, preferred_element_type=F32)
+            dn = dn + lax.dot_general(du, lift_w, NT, preferred_element_type=F32)
+            if first and block == 0:
+                acc_out[rows, :] = out
+                acc_dn[rows, :] = dn
+            else:
+                acc_out[rows, :] += out
+                acc_dn[rows, :] += dn
+
+        grad = lax.dot_general(x[...], dgu[...], TN, preferred_element_type=F32).astype(BF16)
+        gu[block] = grad[:, :width].reshape(4, ROWS, width)
+        gu[2 + block] = grad[:, width:].reshape(4, ROWS, width)
+        grad = lax.dot_general(act[...], dy[...], TN, preferred_element_type=F32).astype(BF16)
+        gd[block] = grad.reshape(4, width // 4, D)
+
+    copies = []
+    for q, ref in enumerate(gu_out):
+        for r in range(4):
+            copies.append(
+                pltpu.make_async_copy(
+                    gu.at[jnp.bitwise_xor(p, q), jnp.bitwise_xor(f, r)], ref.at[r], sem
+                )
+            )
+    for q, ref in enumerate(gd_out):
+        for t in range(2):
+            block = jnp.bitwise_xor(jnp.bitwise_and(f, 1), t)
+            copies.append(
+                pltpu.make_async_copy(gd.at[block, jnp.bitwise_xor(p, q)], ref.at[t], sem)
+            )
+    for copy in copies:
+        copy.start()
+    out_own[...] = acc_out[:TOK_DEV, :]
+    dn_own[...] = acc_dn[:TOK_DEV, :]
+    out_oth[...] = acc_out[TOK_DEV:, :].astype(out_oth.dtype)
+    dn_oth[...] = acc_dn[TOK_DEV:, :].astype(dn_oth.dtype)
+    for copy in copies:
+        copy.wait()
+
+
+def mlp_chunk(place, chunk, tokens, weights, carried):
+    start_col, width = CHUNKS[chunk]
+    last = chunk == len(CHUNKS) - 1
+    first = chunk == 0
+    x_own, x_oth, dy_own, dy_oth = tokens
+    gate_up_own, up_pieces, down_pieces = weights
+    side = jax.ShapeDtypeStruct((TOK_DEV, D), BF16 if last else F32)
+    main = jax.ShapeDtypeStruct((TOK_DEV, D), F32)
+    part = jax.ShapeDtypeStruct((4, ROWS, width), BF16)
+    down = jax.ShapeDtypeStruct((2, width // 4, D), BF16)
+    operands = [place, x_own, x_oth, dy_own, dy_oth, gate_up_own, *up_pieces, *down_pieces]
+    if not first:
+        operands += list(carried)
+    flops = 2 * 2 * TOK_DEV * D * 2 * width * 9
+    out = pl.pallas_call(
+        functools.partial(mlp_kernel, first, last, start_col),
+        out_shape=[main, side, main, side] + [part] * 4 + [down] * 4,
+        in_specs=[SMEM] + [ANY] * (len(operands) - 1),
+        out_specs=[VMEM] * 4 + [ANY] * 8,
+        scratch_shapes=[
+            pltpu.VMEM((4, 4, ROWS, width), BF16),
+            pltpu.VMEM((2, 4, width // 4, D), BF16),
+            pltpu.VMEM((2 * TOK_DEV, width), BF16),
+            pltpu.VMEM((2 * TOK_DEV, 2 * width), BF16),
+            pltpu.VMEM((4, 4, ROWS, width), BF16),
+            pltpu.VMEM((2, 4, width // 4, D), BF16),
+            pltpu.VMEM((2 * TOK_DEV, D), BF16),
+            pltpu.VMEM((2 * TOK_DEV, D), BF16),
+            pltpu.VMEM((2 * TOK_DEV, D), F32),
+            pltpu.VMEM((2 * TOK_DEV, D), F32),
+            pltpu.SemaphoreType.DMA(()),
+        ],
+        compiler_params=pltpu.CompilerParams(vmem_limit_bytes=VMEM_LIMIT),
+        cost_estimate=pl.CostEstimate(
+            flops=flops, bytes_accessed=20_000_000, transcendentals=4 * TOK_DEV * width
+        ),
+    )(*operands)
+    return out[:4], out[4:8], out[8:12]
+
+
+def finish_up_kernel(place, *refs):
+    full = refs[-1]
+    p, k = place[0], place[1]
+    position = 0
+    for start_col, width in CHUNKS:
+        for other in range(2):
+            kk = jnp.bitwise_xor(k, other)
+            for q in range(4):
+                pp = jnp.bitwise_xor(p, q)
+                col = (
+                    jnp.right_shift(pp, 1) * FF
+                    + kk * FF_HALF
+                    + jnp.bitwise_and(pp, 1) * FF_SHARD
+                    + start_col
+                )
+                full[:, pl.ds(pl.multiple_of(col, 128), width)] = refs[position][...].astype(F32)
+                position += 1
+
+
+def finish_up(place, pieces):
+    return pl.pallas_call(
+        finish_up_kernel,
+        out_shape=jax.ShapeDtypeStruct((ROWS, 2 * FF), F32),
+        in_specs=[SMEM] + [VMEM] * len(pieces),
+        out_specs=VMEM,
+        compiler_params=pltpu.CompilerParams(vmem_limit_bytes=VMEM_LIMIT),
+        cost_estimate=pl.CostEstimate(flops=0, bytes_accessed=12 * ROWS * FF, transcendentals=0),
+    )(place, *pieces)
+
+
+def finish_down_kernel(place, *refs):
+    full = refs[-1]
+    p, k = place[0], place[1]
+    position = 0
+    for start_col, width in CHUNKS:
+        for other in range(2):
+            kk = jnp.bitwise_xor(k, other)
+            for q in range(4):
+                pp = jnp.bitwise_xor(p, q)
+                row = start_col + pp * (width // 4) + kk * (width // 8)
+                full[pl.ds(pl.multiple_of(row, 16), width // 8), :] = refs[position][...].astype(F32)
+                position += 1
+
+
+def finish_down(place, pieces):
+    return pl.pallas_call(
+        finish_down_kernel,
+        out_shape=jax.ShapeDtypeStruct((FF_SHARD, D), F32),
+        in_specs=[SMEM] + [VMEM] * len(pieces),
+        out_specs=VMEM,
+        compiler_params=pltpu.CompilerParams(vmem_limit_bytes=VMEM_LIMIT),
+        cost_estimate=pl.CostEstimate(flops=0, bytes_accessed=6 * FF_SHARD * D, transcendentals=0),
+    )(place, *pieces)
+
+
 def block_scores(query_groups, key_block, key_offset, query_index, query_docs, token_docs):
     row_count = key_block.shape[0]
     raw = jnp.einsum("qhgd,khd->hgqk", query_groups, key_block, preferred_element_type=jnp.float32)
@@ -60,27 +475,99 @@
     return (raw * HEAD_DIM ** (-0.5), allowed[None, None])
 
 
+def native(s, f):
+    return (f >> 1) == (s & 1)
+
+
+def foreign(s, f):
+    return not native(s, f)
+
+
 def shards(
-    tokens, cotangent, positions, doc_ids, gain_attn, w_qkv, w_out, gain_mlp, w_gate_up, w_down
+    links,
+    tokens,
+    cotangent,
+    positions,
+    doc_ids,
+    gain_attn,
+    w_qkv,
+    w_out,
+    gain_mlp,
+    w_gate_up,
+    w_down,
 ):
+    seq_at, ctx_at, f = (lax.axis_index(name) for name in AXES)
+    k = jnp.bitwise_and(seq_at, 1)
+    p = 2 * jnp.right_shift(seq_at, 1) + jnp.bitwise_and(ctx_at, 1)
+    place = jnp.stack([p, k, f]).astype(jnp.int32)
+    is_native = jnp.right_shift(f, 1) == k
+
+    def row_slice(weight):
+        padded = jnp.pad(weight, ((0, ROWS_PAD - ROWS), (0, 0)))
+        return lax.dynamic_slice_in_dim(padded, k * 128 + p * SLICE, SLICE, 0)
+
+    def gather_rows(weight, *earlier):
+        return links.gather_z(after(row_slice(weight), *earlier))
+
+    gains = jnp.stack([gain_attn, gain_mlp])
+    gain_pieces = [gains] + [links.swap(gains, df=bits) for bits in (1, 2, 3)]
+    gain_rows = jnp.stack(gain_pieces)
+    gain_rows = jnp.stack(
+        [lax.dynamic_index_in_dim(gain_rows, jnp.bitwise_xor(f, z), 0, False) for z in range(4)]
+    )
+    gain_one = gain_rows[:, 0].reshape(D).astype(F32)
+    gain_two = gain_rows[:, 1].reshape(D).astype(F32)
+
+    dy_own = cotangent[0]
+    qkv_z = gather_rows(w_qkv)
+    out_z = gather_rows(w_out, qkv_z)
+    qkv_mine = links.gather_plane(qkv_z)
+    qkv_theirs = [links.core(piece) for piece in qkv_mine]
+    qkv_full = assemble_rows(place, w_qkv, qkv_mine, qkv_theirs)
+    out_mine = links.gather_plane(after(out_z, *qkv_mine))
+    out_theirs = [links.core(piece) for piece in out_mine]
+    out_full = assemble_rows(place, w_out, out_mine, out_theirs)
+    dy_oth = links.core(dy_own)
+
+    chunk_weights = []
+    before_z = (out_z,)
+    before_plane = tuple(out_mine)
+    for chunk, (start_col, width) in enumerate(CHUNKS):
+        col = (
+            jnp.right_shift(p, 1) * FF
+            + k * FF_HALF
+            + jnp.bitwise_and(p, 1) * FF_SHARD
+            + start_col
+        )
+        up_own = after(lax.dynamic_slice_in_dim(w_gate_up, col, width, 1), *before_z)
+        up_z = links.gather_z(up_own)
+        short = width // 4
+        down_own = lax.dynamic_slice_in_dim(w_down, start_col + p * short, short, 0)
+        down_own = after(down_own, *before_z)
+        down_1 = links.swap(down_own, df=1, only=native)
+        down_2 = links.swap(down_own, ds=1, df=2, only=foreign)
+        down_3 = links.swap(down_own, ds=1, df=3, only=foreign)
+        down_z = jnp.stack(
+            [jnp.where(is_native, down_own, down_2), jnp.where(is_native, down_1, down_3)]
+        )
+        before_z = (up_z, down_z)
+        up_z = after(up_z, *before_plane)
+        down_z = after(down_z, *before_plane)
+        first = 1 if chunk % 2 == 0 else 2
+        up_pieces = links.gather_plane(up_z, first)
+        down_pieces = links.gather_plane(down_z, first)
+        before_plane = tuple(up_pieces + down_pieces)
+        chunk_weights.append((w_gate_up, up_pieces, down_pieces))
+
     groups = HEADS // KV_HEADS
     seq_length = doc_ids.shape[1] * BLK
-    row_start = lax.axis_index("ctx") * TOK_DEV
+    row_start = ctx_at * TOK_DEV
     query_index = row_start + jnp.arange(TOK_DEV, dtype=jnp.int32)
     token_docs = jnp.repeat(doc_ids[0], BLK)
     query_docs = lax.dynamic_slice_in_dim(token_docs, row_start, TOK_DEV)
-    full_weights = (
-        lax.all_gather(gain_attn, "fsdp", axis=0, tiled=True),
-        lax.all_gather(w_qkv, "fsdp", axis=0, tiled=True),
-        lax.all_gather(w_out, "fsdp", axis=0, tiled=True),
-        lax.all_gather(gain_mlp, "fsdp", axis=0, tiled=True),
-        lax.all_gather(w_gate_up, "fsdp", axis=0, tiled=True),
-        lax.all_gather(w_down, "fsdp", axis=0, tiled=True),
-    )
-    gain_one, qkv_full, out_full, gain_two, gate_up_full, down_full = full_weights
     source = tokens[0].astype(jnp.float32)
     scale_attn = rms_scale(source)
-    normed = (source * scale_attn * gain_one.astype(jnp.float32)).astype(jnp.bfloat16)
+    normed = (source * scale_attn * gain_one).astype(jnp.bfloat16)
     mixed = jnp.dot(normed, qkv_full, preferred_element_type=jnp.float32)
     angles = positions[0].astype(jnp.float32)[:, None] * frequencies()[None, :]
     queries_b = rotate(mixed[:, :D].reshape(TOK_DEV, HEADS, HEAD_DIM), angles).astype(jnp.bfloat16)
@@ -126,36 +613,44 @@
     attended_b = attn_groups.reshape(TOK_DEV, D).astype(jnp.bfloat16)
     hidden = source + jnp.dot(attended_b, out_full, preferred_element_type=jnp.float32)
     scale_mlp = rms_scale(hidden)
-    normed_mlp = (hidden * scale_mlp * gain_two.astype(jnp.float32)).astype(jnp.bfloat16)
-    gate_up = jnp.dot(normed_mlp, gate_up_full, preferred_element_type=jnp.float32)
-    gate_part = gate_up[:, :FF]
-    up_part = gate_up[:, FF:]
-    silu_gate = jax.nn.silu(gate_part)
-    activated = (silu_gate * up_part).astype(jnp.bfloat16)
-    result = hidden + jnp.dot(activated, down_full, preferred_element_type=jnp.float32)
+    normed_mlp = (hidden * scale_mlp * gain_two).astype(jnp.bfloat16)
+
+    x_oth = links.core(normed_mlp)
+    mlp_tokens = (normed_mlp, x_oth, dy_own, dy_oth)
+    carried = None
+    up_done, down_done = [], []
+    for chunk, (start_col, width) in enumerate(CHUNKS):
+        carried, up_grads, down_grads = mlp_chunk(
+            place, chunk, mlp_tokens, chunk_weights[chunk], carried
+        )
+        first = 1 if chunk % 2 == 0 else 2
+        down_sum = links.reduce_plane(down_grads, first)
+        arrived_1 = links.swap(down_sum[1], df=1, only=native)
+        arrived_2 = links.swap(down_sum[0], ds=1, df=2, only=foreign)
+        arrived_3 = links.swap(down_sum[1], ds=1, df=3, only=foreign)
+        down_sum = jnp.where(is_native, down_sum[0], arrived_2).astype(F32) + jnp.where(
+            is_native, arrived_1, arrived_3
+        ).astype(F32)
+        down_sum = down_sum.astype(BF16)
+        part = width // 8
+        halves = down_sum.reshape(2, part, D)
+        keep = lax.dynamic_index_in_dim(halves, k, 0, False)
+        give = lax.dynamic_index_in_dim(halves, 1 - k, 0, False)
+        down_part = (keep.astype(F32) + links.core(give).astype(F32)).astype(BF16)
+        pieces = links.gather_plane(down_part, 3 - first)
+        down_done += pieces + [links.core(piece) for piece in pieces]
+        up_sum = links.reduce_z(links.reduce_plane(up_grads, first))
+        pieces = links.gather_plane(up_sum, 3 - first)
+        up_done += pieces + [links.core(piece) for piece in pieces]
+    grad_gate_up = finish_up(place, up_done)
+    grad_down = finish_down(place, down_done)
+    out_own, out_oth, dn_own, dn_oth = carried
+    result = hidden + out_own + links.core(out_oth).astype(F32)
     output = result.astype(jnp.bfloat16)[None]
-    back_weights = (
-        lax.all_gather(gain_attn, "fsdp", axis=0, tiled=True),
-        lax.all_gather(w_qkv, "fsdp", axis=0, tiled=True),
-        lax.all_gather(w_out, "fsdp", axis=0, tiled=True),
-        lax.all_gather(gain_mlp, "fsdp", axis=0, tiled=True),
-        lax.all_gather(w_gate_up, "fsdp", axis=0, tiled=True),
-        lax.all_gather(w_down, "fsdp", axis=0, tiled=True),
-    )
-    gain_one, qkv_full, out_full, gain_two, gate_up_full, down_full = back_weights
-    grad_out_b = cotangent[0]
-    d_activated = jnp.dot(grad_out_b, down_full.T, preferred_element_type=jnp.float32)
-    grad_down = jnp.dot(activated.T, grad_out_b, preferred_element_type=jnp.float32)
-    sigmoid_gate = jax.nn.sigmoid(gate_part)
-    d_gate = d_activated * up_part * sigmoid_gate * (1.0 + gate_part * (1.0 - sigmoid_gate))
-    d_up = d_activated * silu_gate
-    d_gate_up = jnp.concatenate([d_gate, d_up], axis=-1).astype(jnp.bfloat16)
-    grad_gate_up = jnp.dot(normed_mlp.T, d_gate_up, preferred_element_type=jnp.float32)
-    d_normed_mlp = jnp.dot(d_gate_up, gate_up_full.T, preferred_element_type=jnp.float32)
-    d_from_norm, grad_gain_mlp = norm_backward(
-        hidden, scale_mlp, gain_two.astype(jnp.float32), d_normed_mlp
-    )
-    d_hidden = grad_out_b.astype(jnp.float32) + d_from_norm
+    d_normed_mlp = dn_own + links.core(dn_oth).astype(F32)
+
+    d_from_norm, grad_gain_mlp = norm_backward(hidden, scale_mlp, gain_two, d_normed_mlp)
+    d_hidden = dy_own.astype(jnp.float32) + d_from_norm
     d_hidden_b = d_hidden.astype(jnp.bfloat16)
     grad_out_proj = jnp.dot(attended_b.T, d_hidden_b, preferred_element_type=jnp.float32)
     d_attended = jnp.dot(d_hidden_b, out_full.T, preferred_element_type=jnp.float32).astype(
@@ -165,10 +660,6 @@
     row_delta = jnp.transpose(
         jnp.sum(d_out_groups.astype(jnp.float32) * attn_groups, axis=-1), (1, 2, 0)
     )
-    key_value_all = lax.all_gather(key_value, "ctx", axis=0, tiled=True)
-    block_total = seq_length // TOK_DEV
-    all_slabs = key_value_all.reshape(block_total, TOK_DEV, 2 * KV_DIM)
-    all_offsets = TOK_DEV * jnp.arange(block_total, dtype=jnp.int32)
 
     def back_block(d_query, item):
         block_rows, key_offset = item
@@ -202,7 +693,7 @@
         )
 
     d_query_zero = jnp.zeros((TOK_DEV, KV_HEADS, groups, HEAD_DIM), jnp.float32)
-    d_query, key_terms = lax.scan(back_block, d_query_zero, (all_slabs, all_offsets))
+    d_query, key_terms = lax.scan(back_block, d_query_zero, (slabs, offsets))
     key_grads = lax.psum_scatter(
         key_terms.reshape(seq_length, 2 * KV_DIM).astype(jnp.bfloat16),
         "ctx",
@@ -218,39 +709,31 @@
     )
     grad_qkv = jnp.dot(normed.T, d_mixed, preferred_element_type=jnp.float32)
     d_normed = jnp.dot(d_mixed, qkv_full.T, preferred_element_type=jnp.float32)
-    d_source, grad_gain_attn = norm_backward(
-        source, scale_attn, gain_one.astype(jnp.float32), d_normed
-    )
+    d_source, grad_gain_attn = norm_backward(source, scale_attn, gain_one, d_normed)
     input_grad = (d_hidden + d_source).astype(jnp.bfloat16)[None]
-    owned = (
-        lax.psum_scatter(
-            grad_gain_attn.astype(jnp.bfloat16), "fsdp", scatter_dimension=0, tiled=True
-        ).astype(jnp.float32),
-        lax.psum_scatter(
-            grad_qkv.astype(jnp.bfloat16), "fsdp", scatter_dimension=0, tiled=True
-        ).astype(jnp.float32),
-        lax.psum_scatter(
-            grad_out_proj.astype(jnp.bfloat16), "fsdp", scatter_dimension=0, tiled=True
-        ).astype(jnp.float32),
-        lax.psum_scatter(
-            grad_gain_mlp.astype(jnp.bfloat16), "fsdp", scatter_dimension=0, tiled=True
-        ).astype(jnp.float32),
-        lax.psum_scatter(
-            grad_gate_up.astype(jnp.bfloat16), "fsdp", scatter_dimension=0, tiled=True
-        ).astype(jnp.float32),
-        lax.psum_scatter(
-            grad_down.astype(jnp.bfloat16), "fsdp", scatter_dimension=0, tiled=True
-        ).astype(jnp.float32),
-    )
-    summed = (
-        lax.psum(owned[0].astype(jnp.bfloat16), ("seq", "ctx")).astype(jnp.float32),
-        lax.psum(owned[1].astype(jnp.bfloat16), ("seq", "ctx")).astype(jnp.float32),
-        lax.psum(owned[2].astype(jnp.bfloat16), ("seq", "ctx")).astype(jnp.float32),
-        lax.psum(owned[3].astype(jnp.bfloat16), ("seq", "ctx")).astype(jnp.float32),
-        lax.psum(owned[4].astype(jnp.bfloat16), ("seq", "ctx")).astype(jnp.float32),
-        lax.psum(owned[5].astype(jnp.bfloat16), ("seq", "ctx")).astype(jnp.float32),
-    )
-    return (output, input_grad, summed[0], summed[1], summed[2], summed[3], summed[4], summed[5])
+
+    def reduce_rows(grad, first):
+        mine, theirs = scatter_rows(place, grad.astype(BF16))
+        arrived = [links.core(piece) for piece in theirs]
+        mine = [(a.astype(F32) + b.astype(F32)).astype(BF16) for a, b in zip(mine, arrived)]
+        total = links.reduce_z(links.reduce_plane(mine, first))
+        pieces = links.gather_plane(total, 3 - first)
+        return finish_rows(place, pieces, [links.core(piece) for piece in pieces])
+
+    grad_out = reduce_rows(grad_out_proj, 1)
+    pair = jnp.stack([grad_gain_attn, grad_gain_mlp], axis=1)
+    widened = jnp.concatenate([grad_qkv, pair], axis=1)
+    reduced = reduce_rows(widened, 2)
+    return (
+        output,
+        input_grad,
+        reduced[:, QKV],
+        reduced[:, :QKV],
+        grad_out,
+        reduced[:, QKV + 1],
+        grad_gate_up,
+        grad_down,
+    )
 
 
 def solution(mesh):
@@ -266,8 +749,9 @@
         P("fsdp", None),
         P("fsdp", None),
     )
+    links = Links([mesh.shape[name] for name in AXES])
     return jax.shard_map(
-        shards,
+        functools.partial(shards, links),
         mesh=mesh,
         in_specs=placed,
         out_specs=(

time: 1030 us -> 626 us (0.61)
  waiting for transfers between devices: 709 us -> 143 us
  starting transfers between devices: 0.79 us -> 131 us
  Pallas kernels: 0 us -> 80.3 us
  matrix products: 166 us -> 111 us
  blocking collectives: 39.2 us -> 0 us
  local copies, waits for them, and re-layouts: 44 us -> 64.9 us
  other arithmetic: 44.4 us -> 63.1 us
    all_gather x4 -> x0, waiting for transfers between devices: 277 us -> none  [the longest x1 148 us: shards(): lax.all_gather(w_gate_up, 'fsdp', axis=0, tiled=True)]
    reduce_scatter x3 -> x0, waiting for transfers between devices: 276 us -> none  [the longest x1 170 us: shards(): lax.psum_scatter(grad_gate_up.astype(jnp.bfloat16), 'fsdp', scatter_dimen...]
    ppermute x0 -> x139, waiting for transfers between devices: none -> 143 us  [swap(): return lax.ppermute(value, AXES, pairs)]
    ppermute x0 -> x139, starting transfers between devices: none -> 131 us  [swap(): return lax.ppermute(value, AXES, pairs)]
    pallas_call x0 -> x10, Pallas kernels: none -> 80.3 us  [the longest x2 51.8 us: mlp_chunk(): pl.pallas_call(functools.partial(mlp_kernel, first, last, start_col), out...]
    unnamed x12 -> x2, waiting for transfers between devices: 79.9 us -> 0.03 us
    psum x1 -> x0, waiting for transfers between devices: 55.4 us -> none  [shards(): lax.psum(owned[1].astype(jnp.bfloat16), ('seq', 'ctx')).astype(jnp.float32)]
    dot_general x6 -> x0, matrix products: 52.9 us -> none  [the longest x1 11.5 us: shards(): jnp.dot(normed_mlp.T, d_gate_up, preferred_element_type=jnp.float32)]
  transfers between devices with their start and end apart: 11 -> 141, of which waited for: 10 -> 37; matrix products, arithmetic and copies ran while one was open for 13% -> 37% of each run, Pallas kernels for 0% -> 13%
where the time goes in v1:
time: 626 us; the launch traced here: 619 us
  waiting for transfers between devices  143 us (23%)
  starting transfers between devices  131 us (21%)
  matrix products  111 us (18%)
  Pallas kernels  80.3 us (13%)
  local copies, waits for them, and re-layouts  64.9 us (10%)
  other arithmetic  63.1 us (10%)
  between operations  16.2 us (3%)
  loops' own time  8.43 us (1%)
    ppermute x139, waiting for transfers between devices, swap(): return lax.ppermute(value, AXES, pairs)  143 us
    ppermute x139, starting transfers between devices, swap(): return lax.ppermute(value, AXES, pairs)  131 us
    pallas_call x2, Pallas kernels, mlp_chunk(): pl.pallas_call(functools.partial(mlp_kernel, first, last, start_col), out...  51.8 us
    dot_general x4, matrix products, block_scores(): jnp.einsum('qhgd,khd->hgqk', query_groups, key_block, preferred_element_t...  29.2 us
    dot_general x2, matrix products, one_block(): jnp.einsum('hgqk,khd->qhgd', expo.astype(jnp.bfloat16), value_block, pref...  17.8 us
    dot_general x2, matrix products, back_block(): jnp.einsum('hgqk,qhgd->khd', probability.astype(jnp.bfloat16), d_out_grou...  17.5 us
    reduce_sum x2, other arithmetic, one_block(): totals = totals * decay + jnp.sum(expo, axis=-1)  17.3 us
    dot_general x2, matrix products, back_block(): jnp.einsum('qhgd,khd->hgqk', d_out_groups, value_block, preferred_element...  17.1 us
  transfers between devices with their start and end apart: 141, of which 37 were waited for; matrix products, arithmetic and copies ran while one was open for 37% of the time, Pallas kernels for 13%

profile of v1, /device:TPU:0, one launch (start us, length us, event | category | flops | bytes accessed | tf_op | source)
XLA Modules:
  0.0 618.8 jit_solution(7441583605991602281)
XLA Ops:
  73.3 8.2 %collective-permute-done.29 = bf16[64,960]{1,0:T(8,128)(2,1)S(1)} collective-permute-done((bf16[64,960]{1,0:T(8,128)(2,1)S(1)}, bf16[64,960]{1,0:T(8,128)(2,1)S(1)}, u32[]{:S(2)}, u32[]{:S(2)}) %collective-permute-start.29) | collective-permute-done | bytes 122912 | tf_op jit(solution)/shard_map/ppermute | solution.py:90
  86.5 7.2 %collective-permute-done.18.m3 = bf16[3,32,960]{2,1,0:T(8,128)(2,1)S(1)} collective-permute-done((bf16[3,32,960]{2,1,0:T(8,128)(2,1)S(1)}, bf16[3,32,960]{2,1,0:T(8,128)(2,1)S(1)}, u32[]{:S(2)}, u32[]{:S(2)}) %collective-permute-start.18) | collective-permute-done | bytes 184352 | tf_op jit(solution)/shard_map/ppermute | solution.py:90
  109.7 56.4 %while.28 = (s32[]{:T(128)}, f32[5,3,512]{2,1,0:T(4,128)S(1)}, f32[5,3,512]{2,1,0:T(4,128)S(1)}, f32[512,5,3,64]{0,3,2,1:T(8,128)}, s32[2]{0:T(128)S(1)}, /*inde...) while((s32[]{:T(128)}, f32[5,3,512]{2,1,0:T(4,128)S(1)}, ...), condition=%wide.region_4.5_spmd.clone, body=%wide.region_1.4_spmd.clone.sunk | while | flops 1052194816 | bytes 56934604 | solution.py:610
  113.4 6.8 %fusion.134 = (f32[5,3,512]{2,1,0:T(4,128)S(1)}, f32[5,512,512,3]{2,1,3,0:T(8,128)}) fusion(pred[512,512]{0,1:T(8,128)(4,1)S(1)} %compare_and_fusion.4, bf16[512,5,64,1]{0,2,3,1:T(8,128)(2,1)S(1)} %bitcast.351, bf16[512,5,3,64]{0,3,2,1:T(8,128)(2,1)S(1)} %get-tuple-element.693), kind=kOutput, calls=%fused_computation.4.clone.1 | convolution fusion | flops 515105280 | bytes 17332224 | tf_op jit(solution)/shard_map/while/body/eval_jaxpr/qhgd,khd->hgqk/dot_general | solution.py:469
  120.2 8.7 %fusion.136 = f32[5,3,512]{2,1,0:T(4,128)S(1)} fusion(f32[5,512,512,3]{2,1,3,0:T(8,128)} %get-tuple-element.640, f32[5,3,512]{2,1,0:T(4,128)S(1)} %get-tuple-element.686, pred[512,512]{0,1:T(8,128)(4,1)S(1)} %compare_and_fusion.4), kind=kLoop, calls=%fused_computation.8.clone.1 | loop fusion | flops 15720960 | bytes 16052224 | tf_op jit(solution)/shard_map/while/body/eval_jaxpr/reduce_sum | solution.py:600
  128.9 8.6 %bitcast_add_fusion.4 = f32[512,5,3,64]{0,3,2,1:T(8,128)} fusion(f32[512,5,3,64]{0,3,2,1:T(8,128)} %get-tuple-element.675, bf16[512,5,64,1]{0,2,3,1:T(8,128)(2,1)S(1)} %bitcast.352, f32[5,512,512,3]{2,1,3,0:T(8,128)} %get-tuple-element.640, f32[5,3,512]{2,1,0:T(4,128)S(1)} %get-tuple-element.686, pred[512,512]{0,1:T(8,128)(4,1)S(1)} %compare_and_fusion.4, ...), kind=kOutput, calls=%fused_computation.11.clone.1 | convolution fusion | flops 520519680 | bytes 20312064 | tf_op jit(solution)/shard_map/while/body/eval_jaxpr/hgqk,khd->qhgd/dot_general | solution.py:601
  148.1 8.7 %fusion.136 = f32[5,3,512]{2,1,0:T(4,128)S(1)} fusion(f32[5,512,512,3]{2,1,3,0:T(8,128)} %get-tuple-element.640, f32[5,3,512]{2,1,0:T(4,128)S(1)} %get-tuple-element.686, pred[512,512]{0,1:T(8,128)(4,1)S(1)} %compare_and_fusion.4), kind=kLoop, calls=%fused_computation.8.clone.1 | loop fusion | flops 15720960 | bytes 16052224 | tf_op jit(solution)/shard_map/while/body/eval_jaxpr/reduce_sum | solution.py:600
  156.8 9.2 %bitcast_add_fusion.4 = f32[512,5,3,64]{0,3,2,1:T(8,128)} fusion(f32[512,5,3,64]{0,3,2,1:T(8,128)} %get-tuple-element.675, bf16[512,5,64,1]{0,2,3,1:T(8,128)(2,1)S(1)} %bitcast.352, f32[5,512,512,3]{2,1,3,0:T(8,128)} %get-tuple-element.640, f32[5,3,512]{2,1,0:T(4,128)S(1)} %get-tuple-element.686, pred[512,512]{0,1:T(8,128)(4,1)S(1)} %compare_and_fusion.4, ...), kind=kOutput, calls=%fused_computation.11.clone.1 | convolution fusion | flops 520519680 | bytes 20312064 | tf_op jit(solution)/shard_map/while/body/eval_jaxpr/hgqk,khd->qhgd/dot_general | solution.py:601
  212.2 14.1 %collective-permute-done.47.d2 = bf16[2,96,960]{2,1,0:T(8,128)(2,1)} collective-permute-done((bf16[2,96,960]{2,1,0:T(8,128)(2,1)}, bf16[2,96,960]{2,1,0:T(8,128)(2,1)}, u32[]{:S(2)}, u32[]{:S(2)}) %collective-permute-start.47) | collective-permute-done | bytes 368672 | tf_op jit(solution)/shard_map/ppermute | solution.py:90
  230.6 20.3 %shard_map.163 = (f32[512,960]{1,0:T(8,128)}, f32[512,960]{1,0:T(8,128)}, f32[512,960]{1,0:T(8,128)}, f32[512,960]{1,0:T(8,128)}, bf16[4,240,256]{2,1,0:T(8,128)...) custom-call(s32[3]{0:T(128)} %pad_add_fusion.place, ...), custom_call_target="tpu_custom_call" | custom-call | flops 9059696640 | bytes 20000000 | tf_op jit(solution)/shard_map/pallas_call | solution.py:386
  254.0 31.5 %shard_map.164 = (f32[512,960]{1,0:T(8,128)}, bf16[512,960]{1,0:T(8,128)(2,1)}, f32[512,960]{1,0:T(8,128)}, bf16[512,960]{1,0:T(8,128)(2,1)}, bf16[4,240,384]{2,...) custom-call(s32[3]{0:T(128)} %pad_add_fusion.place, ...), custom_call_target="tpu_custom_call" | custom-call | flops 13589544960 | bytes 20000000 | tf_op jit(solution)/shard_map/pallas_call | solution.py:386
  299.9 9.6 %collective-permute-done.113 = bf16[2,64,960]{2,1,0:T(8,128)(2,1)S(1)} collective-permute-done((bf16[2,64,960]{2,1,0:T(8,128)(2,1)S(1)}, bf16[2,64,960]{2,1,0:T(8,128)(2,1)S(1)}, u32[]{:S(2)}, u32[]{:S(2)}) %collective-permute-start.113) | collective-permute-done | bytes 245792 | tf_op jit(solution)/shard_map/ppermute | solution.py:90
  325.8 7.0 %collective-permute-done.99 = bf16[4,240,384]{2,1,0:T(8,128)(2,1)S(1)} collective-permute-done((bf16[4,240,384]{2,1,0:T(8,128)(2,1)S(1)}, bf16[4,240,384]{2,1,0:T(8,128)(2,1)S(1)}, u32[]{:S(2)}, u32[]{:S(2)}) %collective-permute-start.99) | collective-permute-done | bytes 737312 | tf_op jit(solution)/shard_map/ppermute | solution.py:90
  342.2 7.6 %collective-permute-start.49 = (bf16[512,960]{0,1:T(8,128)(2,1)}, bf16[512,960]{0,1:T(8,128)(2,1)}, u32[]{:S(2)}, u32[]{:S(2)}) collective-permute-start(bf16[512,960]{0,1:T(8,128)(2,1)} %copy.72), channel_id=1, source_target_pairs={{0,8},{1,9},{2,10},{3,11},{4,12},{5,13},{6,14},{7,15},{8,0},{9,1},... | collective-permute-start | bytes 2949128 | tf_op jit(solution)/shard_map/ppermute | solution.py:90
  369.8 70.4 %while.29 = (s32[]{:T(128)}, f32[512,5,3,64]{0,3,2,1:T(8,128)S(1)}, bf16[2,512,640]{1,2,0:T(8,128)(2,1)}, bf16[2,512,640]{1,2,0:T(8,128)(2,1)}, s32[2]{0:T(128)S...) while((s32[]{:T(128)}, f32[512,5,3,64]{0,3,2,1:T(8,128)S(1)}, ...), condition=%wide.region_9.10_spmd.clone, body=%wide.region_8.9_spmd.clone.sunk | while | flops 2559804416 | bytes 95594760 | solution.py:696
  374.7 7.8 %fusion.149 = f32[5,512,512,3]{2,1,3,0:T(8,128)} fusion(bf16[512,5,64,1]{0,2,3,1:T(8,128)(2,1)S(1)} %bitcast.347, bf16[512,5,3,64]{0,3,2,1:T(8,128)(2,1)S(1)} %get-tuple-element.735), kind=kOutput, calls=%fused_computation.216.clone.1 | convolution fusion | flops 503316480 | bytes 17039360 | tf_op jit(solution)/shard_map/while/body/eval_jaxpr/qhgd,khd->hgqk/dot_general | solution.py:469
  382.5 8.8 %fusion.151 = bf16[5,512,64,1]{1,2,3,0:T(8,128)(2,1)S(1)} fusion(bf16[512,5,3,64]{0,3,2,1:T(8,128)(2,1)} %get-tuple-element.737, f32[5,512,512,3]{2,1,3,0:T(8,128)} %fusion.149, f32[5,3,512]{2,1,0:T(4,128)S(1)} %get-tuple-element.736, pred[512,512]{0,1:T(8,128)(4,1)S(1)} %compare_and_fusion.5), kind=kOutput, calls=%fused_computation.31.clone.1 | convolution fusion | flops 519045120 | bytes 17332224 | tf_op jit(solution)/shard_map/while/body/eval_jaxpr/hgqk,qhgd->khd/dot_general | solution.py:672
  391.3 8.5 %fusion.150 = bf16[5,3,512,512]{2,3,1,0:T(8,128)(2,1)S(1)} fusion(f32[5,512,512,3]{2,1,3,0:T(8,128)} %fusion.149, bf16[512,5,64,1]{0,2,3,1:T(8,128)(2,1)S(1)} %bitcast.353, bf16[512,5,3,64]{0,3,2,1:T(8,128)(2,1)} %get-tuple-element.737, f32[5,3,512]{2,1,0:T(4,128)S(1)} %get-tuple-element.738, f32[5,3,512]{2,1,0:T(4,128)S(1)} %get-tuple-element.736, ...), kind=kOutput, calls=%fused_computation.26.clone.1 | convolution fusion | flops 526909440 | bytes 25227264 | tf_op jit(solution)/shard_map/while/body/eval_jaxpr/qhgd,khd->hgqk/dot_general | solution.py:678
  409.8 7.8 %fusion.149 = f32[5,512,512,3]{2,1,3,0:T(8,128)} fusion(bf16[512,5,64,1]{0,2,3,1:T(8,128)(2,1)S(1)} %bitcast.347, bf16[512,5,3,64]{0,3,2,1:T(8,128)(2,1)S(1)} %get-tuple-element.735), kind=kOutput, calls=%fused_computation.216.clone.1 | convolution fusion | flops 503316480 | bytes 17039360 | tf_op jit(solution)/shard_map/while/body/eval_jaxpr/qhgd,khd->hgqk/dot_general | solution.py:469
  417.5 8.7 %fusion.151 = bf16[5,512,64,1]{1,2,3,0:T(8,128)(2,1)S(1)} fusion(bf16[512,5,3,64]{0,3,2,1:T(8,128)(2,1)} %get-tuple-element.737, f32[5,512,512,3]{2,1,3,0:T(8,128)} %fusion.149, f32[5,3,512]{2,1,0:T(4,128)S(1)} %get-tuple-element.736, pred[512,512]{0,1:T(8,128)(4,1)S(1)} %compare_and_fusion.5), kind=kOutput, calls=%fused_computation.31.clone.1 | convolution fusion | flops 519045120 | bytes 17332224 | tf_op jit(solution)/shard_map/while/body/eval_jaxpr/hgqk,qhgd->khd/dot_general | solution.py:672
  426.3 8.5 %fusion.150 = bf16[5,3,512,512]{2,3,1,0:T(8,128)(2,1)S(1)} fusion(f32[5,512,512,3]{2,1,3,0:T(8,128)} %fusion.149, bf16[512,5,64,1]{0,2,3,1:T(8,128)(2,1)S(1)} %bitcast.353, bf16[512,5,3,64]{0,3,2,1:T(8,128)(2,1)} %get-tuple-element.737, f32[5,3,512]{2,1,0:T(4,128)S(1)} %get-tuple-element.738, f32[5,3,512]{2,1,0:T(4,128)S(1)} %get-tuple-element.736, ...), kind=kOutput, calls=%fused_computation.26.clone.1 | convolution fusion | flops 526909440 | bytes 25227264 | tf_op jit(solution)/shard_map/while/body/eval_jaxpr/qhgd,khd->hgqk/dot_general | solution.py:678
  462.4 6.9 %collective-permute-done.89 = bf16[240,256]{1,0:T(8,128)(2,1)S(1)} collective-permute-done((bf16[240,256]{1,0:T(8,128)(2,1)}, bf16[240,256]{1,0:T(8,128)(2,1)S(1)}, u32[]{:S(2)}, u32[]{:S(2)}) %collective-permute-start.89) | collective-permute-done | bytes 122912 | tf_op jit(solution)/shard_map/ppermute | solution.py:90
  537.8 9.3 %collective-permute-done.102 = bf16[240,384]{1,0:T(8,128)(2,1)S(1)} collective-permute-done((bf16[240,384]{1,0:T(8,128)(2,1)S(1)}, bf16[240,384]{1,0:T(8,128)(2,1)S(1)}, u32[]{:S(2)}, u32[]{:S(2)}) %collective-permute-start.102) | collective-permute-done | bytes 184352 | tf_op jit(solution)/shard_map/ppermute | solution.py:90
  551.8 7.9 %collective-permute-done.93.refs_3_ = bf16[240,256]{1,0:T(8,128)(2,1)S(1)} collective-permute-done((bf16[240,256]{1,0:T(8,128)(2,1)S(1)}, bf16[240,256]{1,0:T(8,128)(2,1)S(1)}, u32[]{:S(2)}, u32[]{:S(2)}) %collective-permute-start.93) | collective-permute-done | bytes 122912 | tf_op jit(solution)/shard_map/ppermute | solution.py:90
  (667 shorter events, 372.3 us)
Async XLA Ops:
  7.2 101.1 %all-gather.2.cloned.1.call-start = ((), (), s32[]{:S(2)}) async-start(), calls=%async_computation.1 | async-start | bytes 1966080 | tf_op jit(solution)/shard_map/all_gather | solution.py:584
  64.0 418.6 %reduce-scatter.2.cloned.1.call-start = ((), (), s32[]{:S(2)}) async-start(), calls=%async_computation.2 | async-start | bytes 1966080 | tf_op jit(solution)/shard_map/reduce_scatter | solution.py:697
  85.2 86.6 %collective-permute-start.33 = (bf16[240,384]{1,0:T(8,128)(2,1)}, bf16[240,384]{1,0:T(8,128)(2,1)}, u32[]{:S(2)}, u32[]{:S(2)}) collective-permute-start(bf16[240,384]{1,0:T(8,128)(2,1)} %constant_dynamic-slice_fusion.3), channel_id=1, source_target_pairs={{0,3},{1,2},{2,1},{3,0},{4,7},{5,6},{6,5},{7,4},{8,11},{9,10},{10,... | collective-permute-start | bytes 552968 | tf_op jit(solution)/shard_map/ppermute | solution.py:90
  97.8 74.6 %collective-permute-start.32 = (bf16[240,384]{1,0:T(8,128)(2,1)}, bf16[240,384]{1,0:T(8,128)(2,1)}, u32[]{:S(2)}, u32[]{:S(2)}) collective-permute-start(bf16[240,384]{1,0:T(8,128)(2,1)} %constant_dynamic-slice_fusion.3), channel_id=1, source_target_pairs={{0,2},{1,3},{2,0},{3,1},{4,6},{5,7},{6,4},{7,5},{8,10},{9,11},{10,... | collective-permute-start | bytes 552968 | tf_op jit(solution)/shard_map/ppermute | solution.py:90
  100.3 73.8 %collective-permute-start.31 = (bf16[240,384]{1,0:T(8,128)(2,1)}, bf16[240,384]{1,0:T(8,128)(2,1)}, u32[]{:S(2)}, u32[]{:S(2)}) collective-permute-start(bf16[240,384]{1,0:T(8,128)(2,1)} %constant_dynamic-slice_fusion.3), channel_id=1, source_target_pairs={{0,1},{1,0},{2,3},{3,2},{4,5},{5,4},{6,7},{7,6},{8,9},{9,8},{10,11... | collective-permute-start | bytes 552968 | tf_op jit(solution)/shard_map/ppermute | solution.py:90
  101.8 72.8 %collective-permute-start.37 = (bf16[2,64,960]{2,1,0:T(8,128)(2,1)S(1)}, bf16[2,64,960]{2,1,0:T(8,128)(2,1)}, u32[]{:S(2)}, u32[]{:S(2)}) collective-permute-start(bf16[2,64,960]{2,1,0:T(8,128)(2,1)S(1)} %pad_maximum_fusion.12.d0), channel_id=1, source_target_pairs={{0,4},{1,5},{2,6},{3,7},{4,0},{5,1},{6,2},{7,3},{8,12},{9,13},{10,... | collective-permute-start | bytes 737288 | tf_op jit(solution)/shard_map/ppermute | solution.py:90
  102.4 73.7 %collective-permute-start.34 = (bf16[3,240,256]{2,1,0:T(8,128)(2,1)S(1)}, bf16[3,240,256]{2,1,0:T(8,128)(2,1)}, u32[]{:S(2)}, u32[]{:S(2)}) collective-permute-start(bf16[3,240,256]{2,1,0:T(8,128)(2,1)S(1)} %pad_maximum_fusion.8.u0), channel_id=1, source_target_pairs={{0,4},{1,5},{2,6},{3,7},{4,0},{5,1},{6,2},{7,3},{8,12},{9,13},{10,... | collective-permute-start | bytes 1105928 | tf_op jit(solution)/shard_map/ppermute | solution.py:90
  178.2 29.6 %collective-permute-start.24 = (bf16[512,960]{0,1:T(8,128)(2,1)}, bf16[512,960]{0,1:T(8,128)(2,1)}, u32[]{:S(2)}, u32[]{:S(2)}) collective-permute-start(bf16[512,960]{0,1:T(8,128)(2,1)} %bitcast.28), channel_id=1, source_target_pairs={{0,8},{1,9},{2,10},{3,11},{4,12},{5,13},{6,14},{7,15},{8,0},{9,1},... | collective-permute-start | bytes 2949128 | tf_op jit(solution)/shard_map/ppermute | solution.py:90
  181.2 47.1 %collective-permute-start.23 = (bf16[512,960]{0,1:T(8,128)(2,1)}, bf16[512,960]{0,1:T(8,128)(2,1)}, u32[]{:S(2)}, u32[]{:S(2)}) collective-permute-start(bf16[512,960]{0,1:T(8,128)(2,1)} %copy.63), channel_id=1, source_target_pairs={{0,8},{1,9},{2,10},{3,11},{4,12},{5,13},{6,14},{7,15},{8,0},{9,1},... | collective-permute-start | bytes 2949128 | tf_op jit(solution)/shard_map/ppermute | solution.py:90
  210.1 41.5 %collective-permute-start.46 = (bf16[2,96,960]{2,1,0:T(8,128)(2,1)}, bf16[2,96,960]{2,1,0:T(8,128)(2,1)}, u32[]{:S(2)}, u32[]{:S(2)}) collective-permute-start(bf16[2,96,960]{2,1,0:T(8,128)(2,1)} %pad_maximum_fusion.7.d0), channel_id=1, source_target_pairs={{0,4},{1,5},{2,6},{3,7},{4,0},{5,1},{6,2},{7,3},{8,12},{9,13},{10,... | collective-permute-start | bytes 1105928 | tf_op jit(solution)/shard_map/ppermute | solution.py:90
  210.5 41.1 %collective-permute-start.40 = (bf16[3,240,384]{2,1,0:T(8,128)(2,1)}, bf16[3,240,384]{2,1,0:T(8,128)(2,1)}, u32[]{:S(2)}, u32[]{:S(2)}) collective-permute-start(bf16[3,240,384]{2,1,0:T(8,128)(2,1)} %pad_maximum_fusion.6.u0), channel_id=1, source_target_pairs={{0,4},{1,5},{2,6},{3,7},{4,0},{5,1},{6,2},{7,3},{8,12},{9,13},{10,... | collective-permute-start | bytes 1658888 | tf_op jit(solution)/shard_map/ppermute | solution.py:90
  250.9 43.3 %collective-permute-start.112 = (bf16[2,64,960]{2,1,0:T(8,128)(2,1)}, bf16[2,64,960]{2,1,0:T(8,128)(2,1)}, u32[]{:S(2)}, u32[]{:S(2)}) collective-permute-start(bf16[2,64,960]{2,1,0:T(8,128)(2,1)} %get-tuple-element.225), channel_id=1, source_target_pairs={{0,4},{1,5},{2,6},{3,7},{4,0},{5,1},{6,2},{7,3},{8,12},{9,13},{10,... | collective-permute-start | bytes 737288 | tf_op jit(solution)/shard_map/ppermute | solution.py:90
  287.6 34.7 %collective-permute-start.125 = (bf16[2,96,960]{2,1,0:T(8,128)(2,1)}, bf16[2,96,960]{2,1,0:T(8,128)(2,1)}, u32[]{:S(2)}, u32[]{:S(2)}) collective-permute-start(bf16[2,96,960]{2,1,0:T(8,128)(2,1)} %get-tuple-element.227), channel_id=1, source_target_pairs={{0,16},{1,17},{2,18},{3,19},{4,20},{5,21},{6,22},{7,23},{8,24},{9,... | collective-permute-start | bytes 1105928 | tf_op jit(solution)/shard_map/ppermute | solution.py:90
  316.0 35.2 %collective-permute-start.85 = (bf16[4,240,256]{2,1,0:T(8,128)(2,1)S(1)}, bf16[4,240,256]{2,1,0:T(8,128)(2,1)S(1)}, u32[]{:S(2)}, u32[]{:S(2)}) collective-permute-start(bf16[4,240,256]{2,1,0:T(8,128)(2,1)S(1)} %copy-done.106), channel_id=1, source_target_pairs={{0,4},{1,5},{2,6},{3,7},{4,0},{5,1},{6,2},{7,3},{8,12},{9,13},{10,... | collective-permute-start | bytes 1474568 | tf_op jit(solution)/shard_map/ppermute | solution.py:90
  319.3 33.7 %collective-permute-start.50 = (bf16[512,960]{0,1:T(8,128)(2,1)S(1)}, bf16[512,960]{0,1:T(8,128)(2,1)}, u32[]{:S(2)}, u32[]{:S(2)}) collective-permute-start(bf16[512,960]{0,1:T(8,128)(2,1)S(1)} %copy-done.23), channel_id=1, source_target_pairs={{0,8},{1,9},{2,10},{3,11},{4,12},{5,13},{6,14},{7,15},{8,0},{9,1},... | collective-permute-start | bytes 2949128 | tf_op jit(solution)/shard_map/ppermute | solution.py:90
  322.3 29.7 %collective-permute-start.87 = (bf16[4,240,256]{2,1,0:T(8,128)(2,1)S(1)}, bf16[4,240,256]{2,1,0:T(8,128)(2,1)S(1)}, u32[]{:S(2)}, u32[]{:S(2)}) collective-permute-start(bf16[4,240,256]{2,1,0:T(8,128)(2,1)S(1)} %add_convert_fusion.4), channel_id=1, source_target_pairs={{0,16},{1,17},{2,18},{3,19},{4,20},{5,21},{6,22},{7,23},{8,24},{9,... | collective-permute-start | bytes 1474568 | tf_op jit(solution)/shard_map/ppermute | solution.py:90
  339.6 139.4 %collective-permute-start.98 = (bf16[4,240,384]{2,1,0:T(8,128)(2,1)}, bf16[4,240,384]{2,1,0:T(8,128)(2,1)}, u32[]{:S(2)}, u32[]{:S(2)}) collective-permute-start(bf16[4,240,384]{2,1,0:T(8,128)(2,1)} %get-tuple-element.219), channel_id=1, source_target_pairs={{0,16},{1,17},{2,18},{3,19},{4,20},{5,21},{6,22},{7,23},{8,24},{9,... | collective-permute-start | bytes 2211848 | tf_op jit(solution)/shard_map/ppermute | solution.py:90
  351.2 128.6 %collective-permute-start.100 = (bf16[4,240,384]{2,1,0:T(8,128)(2,1)}, bf16[4,240,384]{2,1,0:T(8,128)(2,1)}, u32[]{:S(2)}, u32[]{:S(2)}) collective-permute-start(bf16[4,240,384]{2,1,0:T(8,128)(2,1)} %add_convert_fusion.2), channel_id=1, source_target_pairs={{0,4},{1,5},{2,6},{3,7},{4,0},{5,1},{6,2},{7,3},{8,12},{9,13},{10,... | collective-permute-start | bytes 2211848 | tf_op jit(solution)/shard_map/ppermute | solution.py:90
  352.1 102.6 %collective-permute-start.131 = (bf16[48,960]{1,0:T(8,128)(2,1)}, bf16[48,960]{1,0:T(8,128)(2,1)}, u32[]{:S(2)}, u32[]{:S(2)}) collective-permute-start(bf16[48,960]{1,0:T(8,128)(2,1)} %dynamic-slice_bitcast_fusion.2), channel_id=1, source_target_pairs={{0,8},{1,9},{2,10},{3,11},{4,12},{5,13},{6,14},{7,15},{8,0},{9,1},... | collective-permute-start | bytes 276488 | tf_op jit(solution)/shard_map/ppermute | solution.py:90
  476.1 30.5 %collective-permute-start.118 = (bf16[32,960]{1,0:T(8,128)(2,1)}, bf16[32,960]{1,0:T(8,128)(2,1)}, u32[]{:S(2)}, u32[]{:S(2)}) collective-permute-start(bf16[32,960]{1,0:T(8,128)(2,1)} %fusion.70.refs_0_), channel_id=1, source_target_pairs={{0,4},{1,5},{2,6},{3,7},{4,0},{5,1},{6,2},{7,3},{8,12},{9,13},{10,... | collective-permute-start | bytes 184328 | tf_op jit(solution)/shard_map/ppermute | solution.py:90
  476.9 29.8 %collective-permute-start.120 = (bf16[32,960]{1,0:T(8,128)(2,1)}, bf16[32,960]{1,0:T(8,128)(2,1)}, u32[]{:S(2)}, u32[]{:S(2)}) collective-permute-start(bf16[32,960]{1,0:T(8,128)(2,1)} %collective-permute-done.119.refs_2_), channel_id=1, source_target_pairs={{0,4},{1,5},{2,6},{3,7},{4,0},{5,1},{6,2},{7,3},{8,12},{9,13},{10,... | collective-permute-start | bytes 184328 | tf_op jit(solution)/shard_map/ppermute | solution.py:90
  478.2 29.1 %collective-permute-start.68 = (bf16[4,32,960]{2,1,0:T(8,128)(2,1)}, bf16[4,32,960]{2,1,0:T(8,128)(2,1)}, u32[]{:S(2)}, u32[]{:S(2)}) collective-permute-start(bf16[4,32,960]{2,1,0:T(8,128)(2,1)} %get-tuple-element.207), channel_id=1, source_target_pairs={{0,8},{1,9},{2,10},{3,11},{4,12},{5,13},{6,14},{7,15},{8,0},{9,1},... | collective-permute-start | bytes 737288 | tf_op jit(solution)/shard_map/ppermute | solution.py:90
  479.0 28.3 %collective-permute-start.70 = (bf16[4,32,960]{2,1,0:T(8,128)(2,1)}, bf16[4,32,960]{2,1,0:T(8,128)(2,1)}, u32[]{:S(2)}, u32[]{:S(2)}) collective-permute-start(bf16[4,32,960]{2,1,0:T(8,128)(2,1)} %add_convert_fusion.21), channel_id=1, source_target_pairs={{0,4},{1,5},{2,6},{3,7},{4,0},{5,1},{6,2},{7,3},{8,12},{9,13},{10,... | collective-permute-start | bytes 737288 | tf_op jit(solution)/shard_map/ppermute | solution.py:90
  479.8 27.9 %collective-permute-start.74 = (bf16[4,32,960]{2,1,0:T(8,128)(2,1)}, bf16[4,32,960]{2,1,0:T(8,128)(2,1)}, u32[]{:S(2)}, u32[]{:S(2)}) collective-permute-start(bf16[4,32,960]{2,1,0:T(8,128)(2,1)} %add_convert_fusion.18), channel_id=1, source_target_pairs={{0,16},{1,17},{2,18},{3,19},{4,20},{5,21},{6,22},{7,23},{8,24},{9,... | collective-permute-start | bytes 737288 | tf_op jit(solution)/shard_map/ppermute | solution.py:90
  (229 other events, 2842.4 us)
Sparse Core Ops, SparseCore 0:
  64.1 27.3 all-gather.1
  443.0 23.4 reduce-scatter.1
